TPU v7x, 128 devices: a whole 4x4x4 slice. The times are simulated.
128 devices in a mesh: tok: 16 (over y, x_hi, core), src: 8 (over x_lo, z).
Axes of the slice: x: 4 (x_hi: 2, x_lo: 2; x = x_hi * 2 + x_lo), y: 4, z: 4, core: 2. Of those that a mesh axis runs over, the one named last changes fastest.
Arguments:
- hidden_in: bfloat16 [32768, 1024], P(('tok', 'src')), may hold values from -24 to 24
- d_out: bfloat16 [32768, 1024], P(('tok', 'src')), may hold values from -6 to 6
- queries: bfloat16 [32768, 1024], P(('tok', 'src')), may hold values from -160 to 160
- keys: bfloat16 [16, 1024, 1024], P('tok', 'src'), may hold values from -6 to 6
- values: bfloat16 [16, 1024, 1024], P('tok', 'src'), may hold values from -6 to 6
- source_len: int32 [16], replicated, may hold values from 256 to 1024, as said below
- out_weight: bfloat16 [1024, 1024], replicated, may hold values from -0.1875 to 0.1875
- norm_gain: float32 [1024], replicated, may hold values from 0.25 to 1.75
- router: bfloat16 [1024, 128], replicated, may hold values from -0.1875 to 0.1875
- expert_ids: int32 [32768, 2], P(('tok', 'src')), may hold values from 0 to 127, as said below
- expert_slots: int32 [32768, 2], P(('tok', 'src')), may hold values from -1 to 3, as said below
- fc_in: bfloat16 [16, 4096, 1024], P('tok', 'src'), may hold values from -0.1875 to 0.1875
- fc_out: bfloat16 [16, 4096, 1024], P('tok', 'src'), may hold values from -0.09375 to 0.09375
Outputs:
- d_hidden: bfloat16 [32768, 1024], P(('tok', 'src'))
- d_queries: bfloat16 [32768, 1024], P(('tok', 'src'))
- d_keys: bfloat16 [16, 1024, 1024], P('tok', 'src')
- d_values: bfloat16 [16, 1024, 1024], P('tok', 'src')
- d_out_weight: float32 [1024, 1024], P(('tok', 'src'))
- d_router: float32 [1024, 128], replicated
- d_gain: float32 [1024], replicated
- d_fc_in: bfloat16 [16, 4096, 1024], P('tok', 'src')
- d_fc_out: bfloat16 [16, 4096, 1024], P('tok', 'src')
Inputs may be any that keep to these rules, and one draw needn't show every extreme that they name: `source_len`: each document has at least one live source position; the longest document is full and the shortest has 256 positions. `expert_ids`: the two numbers of a token differ; numbers below 16 are the window's experts. `expert_slots`: for a choice of an expert e below 16: its rank among the choices of e made by the 256 tokens of the same device (tokens in order, a token's first choice before its second), or -1 when that rank is 4 or more; -1 for experts outside the window.
All inputs are finite; a program needn't handle non-finite values.
Results may differ from a plain program's by a relative error of at most 0.019.
Values may be sent and summed in bfloat16 or wider, within the bound.
A program may use at most 128 MiB of HBM per device.

v0:
```python
import math

import jax
import jax.numpy as jnp
from jax import lax
from jax.sharding import PartitionSpec as P

HEAD_DIM = 128
CAP = 4


MASKED = -1e30
NORM_EPS = 1e-05
GELU_SCALE = 0.7978845608028654
CUBIC_TERM = 0.044715


def gelu_pair(pre_act):
    tangent = jnp.tanh(GELU_SCALE * (pre_act + CUBIC_TERM * pre_act * pre_act * pre_act))
    gelu_value = 0.5 * pre_act * (1.0 + tangent)
    gelu_slope = 0.5 * (1.0 + tangent) + 0.5 * pre_act * (1.0 - tangent * tangent) * GELU_SCALE * (
        1.0 + 3.0 * CUBIC_TERM * pre_act * pre_act
    )
    return (gelu_value, gelu_slope)


def on_device(
    hidden_in,
    d_out,
    queries,
    keys,
    values,
    source_len,
    out_weight,
    norm_gain,
    router,
    expert_ids,
    expert_slots,
    fc_in,
    fc_out,
):
    tok_rows, model_width = hidden_in.shape
    heads_all = queries.shape[1]
    head_count = heads_all // HEAD_DIM
    tok_count = lax.axis_size("tok")
    factor = 1.0 / math.sqrt(HEAD_DIM)
    doc_index = lax.axis_index("tok")
    length = jnp.sum(jnp.where(jnp.arange(source_len.shape[0]) == doc_index, source_len, 0))
    query_heads = queries.reshape(tok_rows, head_count, HEAD_DIM)
    key_all, value_all = (
        lax.all_gather(keys[0], "src", axis=0, tiled=True),
        lax.all_gather(values[0], "src", axis=0, tiled=True),
    )
    key_all = key_all.reshape(-1, head_count, HEAD_DIM)
    value_all = value_all.reshape(-1, head_count, HEAD_DIM)
    visible = (jnp.arange(key_all.shape[0]) < length)[None, None, :]
    scores = (
        jnp.einsum("thd,shd->hts", query_heads, key_all, preferred_element_type=jnp.float32)
        * factor
    )
    scores = jnp.where(visible, scores, MASKED)
    row_top = jnp.max(scores, axis=2, keepdims=True)
    raised = jnp.where(visible, jnp.exp(scores - row_top), 0.0)
    probs_full = raised / jnp.sum(raised, axis=2, keepdims=True)
    probs_low = probs_full.astype(jnp.bfloat16)
    attended = jnp.einsum("hts,shd->thd", probs_low, value_all, preferred_element_type=jnp.float32)
    attended = attended.astype(jnp.bfloat16).reshape(tok_rows, heads_all)
    mixed = hidden_in.astype(jnp.float32) + jnp.dot(
        attended, out_weight, preferred_element_type=jnp.float32
    )
    row_mean = jnp.mean(mixed, axis=1, keepdims=True)
    centred = mixed - row_mean
    inv_std = lax.rsqrt(jnp.mean(centred * centred, axis=1, keepdims=True) + NORM_EPS)
    normed = centred * inv_std
    expert_in = (normed * norm_gain).astype(jnp.bfloat16)
    columns = jnp.arange(router.shape[1])
    pick_first = (expert_ids[:, 0:1] == columns).astype(jnp.float32)
    pick_second = (expert_ids[:, 1:2] == columns).astype(jnp.float32)
    logits = jnp.dot(expert_in, router, preferred_element_type=jnp.float32)
    first_logit = jnp.sum(logits * pick_first, axis=1)
    second_logit = jnp.sum(logits * pick_second, axis=1)
    first_gate = jax.nn.sigmoid(first_logit - second_logit)
    second_gate = jax.nn.sigmoid(second_logit - first_logit)
    gates_low = lax.optimization_barrier(
        jnp.stack([first_gate, second_gate], axis=1).astype(jnp.bfloat16)
    )
    gates_low = gates_low.astype(jnp.float32)
    slots_all = tok_count * CAP
    slot_lanes = jnp.arange(slots_all)

    def slot_target(id_col, slot_col):
        is_live = (id_col < tok_count) & (slot_col >= 0)
        return jnp.where(is_live, id_col * CAP + slot_col, -1)

    hit_first = (slot_target(expert_ids[:, 0], expert_slots[:, 0])[:, None] == slot_lanes).astype(
        jnp.float32
    )
    hit_second = (slot_target(expert_ids[:, 1], expert_slots[:, 1])[:, None] == slot_lanes).astype(
        jnp.float32
    )
    route_map = hit_first + hit_second
    route_low = route_map.astype(jnp.bfloat16)
    sent_in = jnp.einsum("te,td->ed", route_low, expert_in, preferred_element_type=jnp.float32)
    sent_grad = jnp.einsum("te,td->ed", route_low, d_out, preferred_element_type=jnp.float32)
    sent_gate = jnp.sum(hit_first * gates_low[:, 0:1] + hit_second * gates_low[:, 1:2], axis=0)
    sent_in = sent_in.astype(jnp.bfloat16).reshape(tok_count, CAP, model_width)
    sent_grad = sent_grad.astype(jnp.bfloat16).reshape(tok_count, CAP, model_width)
    sent_gate = sent_gate.astype(jnp.bfloat16).reshape(tok_count, CAP, 1)
    got_in, got_grad, got_gate = (
        lax.all_to_all(sent_in, "tok", split_axis=0, concat_axis=1, tiled=True),
        lax.all_to_all(sent_grad, "tok", split_axis=0, concat_axis=1, tiled=True),
        lax.all_to_all(sent_gate, "tok", split_axis=0, concat_axis=1, tiled=True),
    )
    rows_in, rows_grad, rows_gate = (
        lax.all_gather(got_in, "src", axis=1, tiled=True),
        lax.all_gather(got_grad, "src", axis=1, tiled=True),
        lax.all_gather(got_gate, "src", axis=1, tiled=True),
    )
    x_rows = rows_in[0]
    grad_rows = rows_grad[0]
    gate_rows = rows_gate[0].astype(jnp.float32)
    weight_in = fc_in[0]
    weight_out = fc_out[0]
    pre_act = jnp.einsum("rd,fd->rf", x_rows, weight_in, preferred_element_type=jnp.float32)
    gelu_value, gelu_slope = gelu_pair(pre_act)
    activated = lax.optimization_barrier(gelu_value.astype(jnp.bfloat16))
    back_proj = jnp.einsum("rd,fd->rf", grad_rows, weight_out, preferred_element_type=jnp.float32)
    gate_part = jnp.sum(back_proj * activated.astype(jnp.float32), axis=1, keepdims=True)
    d_pre = (gate_rows * back_proj * gelu_slope).astype(jnp.bfloat16)
    scaled_grad = (gate_rows * grad_rows.astype(jnp.float32)).astype(jnp.bfloat16)
    d_fc_out = jnp.einsum("rf,rd->fd", activated, scaled_grad, preferred_element_type=jnp.float32)
    d_fc_out = d_fc_out.astype(jnp.bfloat16)[None]
    d_fc_in = jnp.einsum("rf,rd->fd", d_pre, x_rows, preferred_element_type=jnp.float32)
    d_fc_in = d_fc_in.astype(jnp.bfloat16)[None]
    input_part = jnp.einsum("rf,fd->rd", d_pre, weight_in, preferred_element_type=jnp.float32)
    input_sum, gate_sum = (
        lax.psum_scatter(input_part, "src", scatter_dimension=0, tiled=True),
        lax.psum_scatter(gate_part, "src", scatter_dimension=0, tiled=True),
    )
    back_in, back_gate = (
        lax.all_to_all(input_sum[None], "tok", split_axis=1, concat_axis=0, tiled=True),
        lax.all_to_all(gate_sum[None], "tok", split_axis=1, concat_axis=0, tiled=True),
    )
    back_in = back_in.reshape(slots_all, model_width)
    back_gate = back_gate.reshape(slots_all)
    moe_grad = jnp.dot(route_map, back_in, precision=lax.Precision.HIGHEST)
    grad_first = jnp.dot(hit_first, back_gate, precision=lax.Precision.HIGHEST)
    grad_second = jnp.dot(hit_second, back_gate, precision=lax.Precision.HIGHEST)
    logit_grad = first_gate * second_gate * (grad_first - grad_second)
    column_grad = (pick_first - pick_second) * logit_grad[:, None]
    total_grad = moe_grad + jnp.dot(
        column_grad, router.astype(jnp.float32).T, precision=lax.Precision.HIGHEST
    )
    router_part = jnp.dot(
        expert_in.astype(jnp.float32).T, column_grad, precision=lax.Precision.HIGHEST
    )
    gain_part = jnp.sum(total_grad * normed, axis=0)
    d_router, d_gain = lax.psum((router_part, gain_part), ("tok", "src"))
    scaled = total_grad * norm_gain
    mixed_grad = d_out.astype(jnp.float32) + inv_std * (
        scaled
        - jnp.mean(scaled, axis=1, keepdims=True)
        - normed * jnp.mean(scaled * normed, axis=1, keepdims=True)
    )
    d_hidden = mixed_grad.astype(jnp.bfloat16)
    out_grad = jnp.einsum("td,hd->th", d_hidden, out_weight, preferred_element_type=jnp.float32)
    out_grad = out_grad.astype(jnp.bfloat16)
    d_out_weight = lax.psum_scatter(
        jnp.einsum("th,td->hd", attended, d_hidden, preferred_element_type=jnp.float32),
        ("tok", "src"),
        scatter_dimension=0,
        tiled=True,
    )
    out_heads = out_grad.reshape(tok_rows, head_count, HEAD_DIM)
    att_heads = attended.reshape(tok_rows, head_count, HEAD_DIM)
    row_term = jnp.einsum("thd,thd->ht", out_heads, att_heads, preferred_element_type=jnp.float32)
    prob_grad = jnp.einsum("thd,shd->hts", out_heads, value_all, preferred_element_type=jnp.float32)
    score_grad = (probs_full * (prob_grad - row_term[:, :, None]) * factor).astype(jnp.bfloat16)
    d_queries = jnp.einsum("hts,shd->thd", score_grad, key_all, preferred_element_type=jnp.float32)
    d_queries = d_queries.astype(jnp.bfloat16).reshape(tok_rows, heads_all)
    key_part = jnp.einsum(
        "hts,thd->shd", score_grad, query_heads, preferred_element_type=jnp.float32
    )
    value_part = jnp.einsum(
        "hts,thd->shd", probs_low, out_heads, preferred_element_type=jnp.float32
    )
    key_sum, value_sum = (
        lax.psum_scatter(
            key_part.reshape(-1, heads_all).astype(jnp.bfloat16),
            "src",
            scatter_dimension=0,
            tiled=True,
        ).astype(jnp.float32),
        lax.psum_scatter(
            value_part.reshape(-1, heads_all).astype(jnp.bfloat16),
            "src",
            scatter_dimension=0,
            tiled=True,
        ).astype(jnp.float32),
    )
    d_keys = key_sum.astype(jnp.bfloat16)[None]
    d_values = value_sum.astype(jnp.bfloat16)[None]
    return (
        d_hidden,
        d_queries,
        d_keys,
        d_values,
        d_out_weight,
        d_router,
        d_gain,
        d_fc_in,
        d_fc_out,
    )


def solution(mesh):
    return jax.shard_map(
        on_device,
        mesh=mesh,
        in_specs=(
            P(("tok", "src"), None),
            P(("tok", "src"), None),
            P(("tok", "src"), None),
            P("tok", "src", None),
            P("tok", "src", None),
            P(),
            P(),
            P(),
            P(),
            P(("tok", "src"), None),
            P(("tok", "src"), None),
            P("tok", "src", None),
            P("tok", "src", None),
        ),
        out_specs=(
            P(("tok", "src"), None),
            P(("tok", "src"), None),
            P("tok", "src", None),
            P("tok", "src", None),
            P(("tok", "src"), None),
            P(),
            P(),
            P("tok", "src", None),
            P("tok", "src", None),
        ),
        check_vma=False,
    )
```

profile of v0, /device:TPU:0, one launch (start us, length us, event | category | flops | bytes accessed | tf_op | source)
XLA Modules:
  0.0 1238.5 jit_solution(8750840995257358089)
XLA Ops:
  14.0 43.9 %all-gather.11.cloned.1.call-done = bf16[1,1024,1024]{1,2,0:T(8,128)(2,1)} async-done(((bf16[1,128,1024]{1,2,0:T(8,128)(2,1)}), bf16[1,1024,1024]{1,2,0:T(8,128)(2,1)}) %all-gather.11.cloned.1.call-update) | async-done | bytes 2097168 | tf_op jit(solution)/shard_map/all_gather | solution.py:51
  57.9 8.1 fusion.58
  66.0 5.3 fusion.5
  71.3 31.4 %all-gather.13.cloned.1.call-done = bf16[1,1024,1024]{2,1,0:T(8,128)(2,1)} async-done(((bf16[1,128,1024]{2,1,0:T(8,128)(2,1)}), bf16[1,1024,1024]{2,1,0:T(8,128)(2,1)}) %all-gather.13.cloned.1.call-update) | async-done | bytes 2097168 | tf_op jit(solution)/shard_map/all_gather | solution.py:52
  106.7 4.4 convolution_convert_fusion.5
  114.3 14.5 %all_to_all.54 = bf16[16,4,1024]{2,1,0:T(4,128)(2,1)S(1)} all-to-all(bf16[16,4,1024]{2,1,0:T(4,128)(2,1)S(1)} %reshape.180), channel_id=1, replica_groups=mesh['tok'=16,'src'=8] {'tok'}, dimensions={0} | all-to-all | bytes 262144 | tf_op jit(solution)/shard_map/all_to_all | solution.py:110
  130.9 10.8 all_to_all.55
  142.5 21.3 %all-gather.9.cloned.1.call-done = bf16[1,512,1024]{2,1,0:T(8,128)(2,1)} async-done(((bf16[1,64,1024]{2,1,0:T(8,128)(2,1)}), bf16[1,512,1024]{2,1,0:T(8,128)(2,1)}) %all-gather.9.cloned.1.call-update) | async-done | bytes 1048592 | tf_op jit(solution)/shard_map/all_gather | solution.py:115
  167.4 36.8 %all-gather.7.cloned.1.call-done = bf16[1,512,1024]{2,1,0:T(8,128)(2,1)} async-done(((bf16[1,64,1024]{2,1,0:T(8,128)(2,1)}), bf16[1,512,1024]{2,1,0:T(8,128)(2,1)}) %all-gather.7.cloned.1.call-update) | async-done | bytes 1048592 | tf_op jit(solution)/shard_map/all_gather | solution.py:116
  209.1 36.0 %reduce-scatter.16.cloned.1.call-done = f32[64,1]{1,0:T(8,128)} async-done(((f32[512,1]{1,0:T(8,128)}), f32[64,1]{1,0:T(8,128)}) %reduce-scatter.16.cloned.1.call-update) | async-done | bytes 272
  246.7 6.5 all-to-all-start.4
  254.6 6.2 all-to-all-done.4
  266.7 6.7 all-to-all-done
  273.9 16.3 %all-reduce = bf16[512]{0:T(512)(128)(2,1)S(1)} all-reduce(bf16[512]{0:T(512)(128)(2,1)S(1)} %dynamic-update-slice), channel_id=1, replica_groups=mesh['tok'=16,'src'=8] {'src'}, use_global_device_ids=true, to_apply=%add | all-reduce | flops 512 | bytes 2048
  296.5 38.7 %reduce-scatter.8.cloned.1.call-done = f32[64,1024]{1,0:T(8,128)} async-done(((f32[512,1024]{1,0:T(8,128)}), f32[64,1024]{1,0:T(8,128)}) %reduce-scatter.8.cloned.1.call-update) | async-done | bytes 262160 | tf_op jit(solution)/shard_map/reduce_scatter | solution.py:137
  337.2 6.4 all-to-all-start.3
  346.3 6.9 all-to-all-done.3
  358.7 4.4 convolution_convert_fusion.1
  372.2 6.2 multiply_convert_fusion
  400.8 62.7 %psum.15 = f32[1024]{0:T(1024)} all-reduce(f32[1024]{0:T(1024)S(1)} %get-tuple-element.54), channel_id=1, replica_groups=mesh['tok'=16,'src'=8] {'tok','src'}, use_global_device_ids=true, to_apply=%region_18.19 | all-reduce | flops 1024 | bytes 8192 | tf_op jit(solution)/shard_map/psum | solution.py:158
  463.5 30.5 %all-reduce.3.cloned.1.call-done = f32[1024,128]{1,0:T(8,128)} async-done(((f32[1024,128]{1,0:T(8,128)}), f32[1024,128]{1,0:T(8,128)}) %all-reduce.3.cloned.1.call-update) | async-done | bytes 524304 | tf_op jit(solution)/shard_map/psum | solution.py:158
  494.0 45.2 %reduce-scatter.12.cloned.1.call-done = bf16[128,1024]{1,0:T(8,128)(2,1)} async-done(((bf16[1024,1024]{1,0:T(8,128)(2,1)}), bf16[128,1024]{1,0:T(8,128)(2,1)}) %reduce-scatter.12.cloned.1.call-update) | async-done | bytes 262160 | tf_op jit(solution)/shard_map/reduce_scatter | solution.py:194
  539.2 44.0 %reduce-scatter.10.cloned.1.call-done = bf16[128,1024]{1,0:T(8,128)(2,1)} async-done(((bf16[1024,1024]{1,0:T(8,128)(2,1)}), bf16[128,1024]{1,0:T(8,128)(2,1)}) %reduce-scatter.10.cloned.1.call-update) | async-done | bytes 262160 | tf_op jit(solution)/shard_map/reduce_scatter | solution.py:188
  583.2 646.6 %reduce-scatter.14.cloned.1.call-done = f32[8,1024]{1,0:T(8,128)} async-done(((f32[1024,1024]{1,0:T(8,128)}), f32[8,1024]{1,0:T(8,128)}) %reduce-scatter.14.cloned.1.call-update) | async-done | bytes 32784 | tf_op jit(solution)/shard_map/reduce_scatter | solution.py:168
  (121 shorter events, 83.1 us)
Async XLA Ops:
  7.2 104.8 %copy-start = (bf16[1024,1024]{1,0:T(8,128)(2,1)S(1)}, bf16[1024,1024]{1,0:T(8,128)(2,1)}, u32[]{:S(2)}) copy-start(bf16[1024,1024]{1,0:T(8,128)(2,1)} %param.19) | copy-start | bytes 6291460
  7.2 50.7 %all-gather.11.cloned.1.call-start = ((), (), s32[]{:S(2)}) async-start(), calls=%async_computation.17 | async-start | bytes 2359296 | tf_op jit(solution)/shard_map/all_gather | solution.py:51
  9.2 93.6 %all-gather.13.cloned.1.call-start = ((), (), s32[]{:S(2)}) async-start(), calls=%async_computation.18 | async-start | bytes 2359296 | tf_op jit(solution)/shard_map/all_gather | solution.py:52
  9.9 153.9 %all-gather.9.cloned.1.call-start = ((), (), s32[]{:S(2)}) async-start(), calls=%async_computation.11 | async-start | bytes 1179648 | tf_op jit(solution)/shard_map/all_gather | solution.py:115
  11.2 54.7 %copy-start.11 = (bf16[256,1024]{0,1:T(8,128)(2,1)}, bf16[256,1024]{0,1:T(8,128)(2,1)S(1)}, u32[]{:S(2)}) copy-start(bf16[256,1024]{0,1:T(8,128)(2,1)S(1)} %copy.132) | copy-start | bytes 1572868
  106.7 5.3 copy-start.14
  129.6 74.7 %all-gather.7.cloned.1.call-start = ((), (), s32[]{:S(2)}) async-start(), calls=%async_computation.10 | async-start | bytes 1179648 | tf_op jit(solution)/shard_map/all_gather | solution.py:116
  142.5 102.7 %reduce-scatter.16.cloned.1.call-start = ((), (), s32[]{:S(2)}) async-start(), calls=%async_computation.19 | async-start | bytes 294912
  167.4 41.1 %copy-start.17 = (u32[128]{0:T(128)S(1)}, u32[128]{0:T(128)}, u32[]{:S(2)}) copy-start(u32[128]{0:T(128)} %constant.52) | copy-start | bytes 1540
  167.4 85.8 %copy-start.15 = (bf16[1024,128]{1,0:T(8,128)(2,1)S(1)}, bf16[1024,128]{1,0:T(8,128)(2,1)}, u32[]{:S(2)}) copy-start(bf16[1024,128]{1,0:T(8,128)(2,1)} %param.21) | copy-start | bytes 786436
  246.7 14.1 %all-to-all-start.4 = ((f32[1,64,1]{2,0,1:T(1,128)}), f32[1,64,1]{2,0,1:T(1,128)S(1)}, u32[]{:S(2)}, u32[]{:S(2)}) async-start(f32[1,64,1]{2,0,1:T(1,128)} %copy.112), calls=%async_computation.5 | async-start | bytes 65536 | tf_op jit(solution)/shard_map/all_to_all | solution.py:142
  262.6 10.9 all-to-all-start
  266.0 69.2 %reduce-scatter.8.cloned.1.call-start = ((), (), s32[]{:S(2)}) async-start(), calls=%async_computation.12 | async-start | bytes 2359296 | tf_op jit(solution)/shard_map/reduce_scatter | solution.py:137
  337.2 16.0 %all-to-all-start.3 = ((f32[1,64,1024]{2,0,1:T(1,128)}), f32[1,64,1024]{2,0,1:T(1,128)S(1)}, u32[]{:S(2)}, u32[]{:S(2)}) async-start(f32[1,64,1024]{2,0,1:T(1,128)} %copy.111), calls=%async_computation.4 | async-start | bytes 524288 | tf_op jit(solution)/shard_map/all_to_all | solution.py:141
  343.6 150.4 %all-reduce.3.cloned.1.call-start = ((), (), s32[]{:S(2)}) async-start(), calls=%async_computation.16 | async-start | bytes 1048576 | tf_op jit(solution)/shard_map/psum | solution.py:158
  346.2 193.0 %reduce-scatter.12.cloned.1.call-start = ((), (), s32[]{:S(2)}) async-start(), calls=%async_computation.14 | async-start | bytes 2359296 | tf_op jit(solution)/shard_map/reduce_scatter | solution.py:194
  358.7 4.5 copy-start.13
  363.1 7.7 copy-start.2
  367.2 216.1 %reduce-scatter.10.cloned.1.call-start = ((), (), s32[]{:S(2)}) async-start(), calls=%async_computation.13 | async-start | bytes 2359296 | tf_op jit(solution)/shard_map/reduce_scatter | solution.py:188
  372.2 8.2 copy-start.12
  382.4 4.3 copy-start.10
  386.4 843.3 %reduce-scatter.14.cloned.1.call-start = ((), (), s32[]{:S(2)}) async-start(), calls=%async_computation.15 | async-start | bytes 4227072 | tf_op jit(solution)/shard_map/reduce_scatter | solution.py:168
  389.4 4.1 copy-start.18
  390.5 6.1 copy-start.5
  (8 other events, 11.2 us)
Sparse Core Ops, SparseCore 0:
  10.2 47.7 all-gather.10
  59.6 43.1 all-gather.12
  129.7 34.1 all-gather.8
  165.9 38.2 all-gather.6
  208.6 36.4 reduce-scatter.15
  296.6 38.5 reduce-scatter.7
  349.9 144.0 all-reduce.2
  497.0 42.2 reduce-scatter.11
  542.2 40.9 reduce-scatter.9
  586.0 643.7 reduce-scatter.13
where the time goes:
time: 1240 us
  waiting for transfers between devices  995 us (80%)
  blocking collectives  104 us (8%)
  matrix products  57.7 us (5%)
  local copies, waits for them, and re-layouts  34.6 us (3%)
  starting transfers between devices  17.1 us (1%)
  between operations  15.2 us (1%)
  other arithmetic  14.4 us (1%)
    reduce_scatter x1, waiting for transfers between devices, on_device(): lax.psum_scatter(jnp.einsum('th,td->hd', attended, d_hidden, preferred_el...  647 us
    psum x1, blocking collectives, on_device(): d_router, d_gain = lax.psum((router_part, gain_part), ('tok', 'src'))  62.7 us
    reduce_scatter x1, waiting for transfers between devices, on_device(): lax.psum_scatter(value_part.reshape(-1, heads_all).astype(jnp.bfloat16),...  45.2 us
    reduce_scatter x1, waiting for transfers between devices, on_device(): lax.psum_scatter(key_part.reshape(-1, heads_all).astype(jnp.bfloat16), 's...  44 us
    all_gather x1, waiting for transfers between devices, on_device(): lax.all_gather(keys[0], 'src', axis=0, tiled=True)  43.9 us
    reduce_scatter x1, waiting for transfers between devices, on_device(): lax.psum_scatter(input_part, 'src', scatter_dimension=0, tiled=True)  38.7 us
    unnamed x11, waiting for transfers between devices  36.9 us
    all_gather x1, waiting for transfers between devices, on_device(): lax.all_gather(got_grad, 'src', axis=1, tiled=True)  36.8 us
  transfers between devices with their start and end apart: 13, of which 13 were waited for; matrix products, arithmetic and copies ran while one was open for 6% of the time, Pallas kernels for 0%

commit v1 on v0

v1 whole, which is shorter than its diff:
```python
import math

import jax
import jax.numpy as jnp
from jax import lax
from jax.experimental import pallas as pl
from jax.experimental.pallas import tpu as pltpu
from jax.sharding import PartitionSpec as P

MESH = pl.DeviceIdType.MESH
BF, F32 = jnp.bfloat16, jnp.float32
HEAD = 128
CAP = 4
NORM_EPS = 1e-05
GELU_SCALE = 0.7978845608028654
CUBIC_TERM = 0.044715
FACTOR = 1.0 / math.sqrt(HEAD)
EXP2_SCALE = FACTOR / math.log(2.0)
MASKED = -1e30
N_SRC, N_TOK = 8, 16
ROWS, WIDTH, SRC_ALL = 256, 1024, 1024


def nn(a, b, **kw):
    return lax.dot_general(a, b, (((1,), (0,)), ((), ())), preferred_element_type=F32, **kw)


def nt(a, b, **kw):
    return lax.dot_general(a, b, (((1,), (1,)), ((), ())), preferred_element_type=F32, **kw)


def src_step(src, k, back=False):
    x, z = src // 4, src % 4
    z = (z + 4 - k % 4) % 4 if back else (z + k % 4) % 4
    return ((x + k // 4) % 2) * 4 + z


def tok_step(tok, k, back=False):
    y, x, c = tok // 4, (tok // 2) % 2, tok % 2
    y = (y + 4 - k // 4) % 4 if back else (y + k // 4) % 4
    return y * 4 + ((x + (k // 2) % 2) % 2) * 2 + (c + k % 2) % 2


def remote(src_ref, dst_ref, send_sem, recv_sem, axis, peer):
    return pltpu.make_async_remote_copy(
        src_ref=src_ref,
        dst_ref=dst_ref,
        send_sem=send_sem,
        recv_sem=recv_sem,
        device_id={axis: peer},
        device_id_type=MESH,
    )


def each(count, body):
    def step(k, carry):
        body(k)
        return carry

    lax.fori_loop(1, count, step, 0)


def greet(src, tok):
    bar = pltpu.get_barrier_semaphore()
    waits = 0
    if src is not None:
        waits += N_SRC - 1
        each(N_SRC, lambda k: pl.semaphore_signal(bar, inc=1, device_id={"src": src_step(src, k)}, device_id_type=MESH))
    if tok is not None:
        waits += N_TOK - 1
        each(N_TOK, lambda k: pl.semaphore_signal(bar, inc=1, device_id={"tok": tok_step(tok, k)}, device_id_type=MESH))
    pl.semaphore_wait(bar, waits)


class Swap:
    def __init__(self, axis, me, sems, source, target):
        self.axis, self.me, self.sems = axis, me, sems
        self.source, self.target = source, target
        self.count = N_SRC if axis == "src" else N_TOK
        self.step = src_step if axis == "src" else tok_step

    def copy(self, k, to, slot):
        return remote(self.source(to), self.target(slot), self.sems.at[0, k], self.sems.at[1, k], self.axis, to)

    def send(self, k):
        self.copy(k, self.step(self.me, k), self.me).start()

    def arrive(self, k):
        sender = self.step(self.me, k, True)
        self.copy(k, sender, sender).wait_recv()

    def sent(self, k):
        self.copy(k, self.step(self.me, k), self.me).wait_send()

    def send_all(self):
        each(self.count, self.send)

    def arrive_all(self):
        each(self.count, self.arrive)

    def sent_all(self):
        each(self.count, self.sent)


def lanes(index):
    return pl.ds(pl.multiple_of(index * HEAD, HEAD), HEAD)


def rows(index, size):
    return pl.ds(pl.multiple_of(index * size, size), size)


def fill_bias(length, bias):
    place = lax.broadcasted_iota(jnp.int32, bias.shape, 0)
    bias[...] = jnp.where(place < length, 0.0, MASKED)


def fold8(value, op):
    return op(value.reshape(value.shape[0] // 8, 8, value.shape[1]), axis=0)


def attend_kernel(
    q_ref, k_ref, v_ref, len_ref,
    att_out, qh_out, kh_out, vh_out, oT_out, stat_out,
    qh, kh, vh, att_in, att_send, vT, sbuf, pbuf, bias,
    k_sem, v_sem, q_sem, a_sem,
):
    src, tok = lax.axis_index("src"), lax.axis_index("tok")
    greet(src, None)
    k_swap = Swap("src", src, k_sem, lambda p: k_ref.at[:, lanes(p)], lambda i: kh.at[rows(i, 128)])
    v_swap = Swap("src", src, v_sem, lambda p: v_ref.at[:, lanes(p)], lambda i: vh.at[rows(i, 128)])
    q_swap = Swap("src", src, q_sem, lambda p: q_ref.at[:, lanes(p)], lambda i: qh.at[i])
    a_swap = Swap("src", src, a_sem, lambda p: att_send.at[p], lambda i: att_in.at[i])
    k_swap.send_all()
    v_swap.send_all()
    q_swap.send_all()
    kh[rows(src, 128), :] = k_ref[:, lanes(src)]
    vh[rows(src, 128), :] = v_ref[:, lanes(src)]
    qh[src] = q_ref[:, lanes(src)]
    fill_bias(len_ref[tok], bias)
    k_swap.arrive_all()
    v_swap.arrive_all()
    vT[...] = vh[...].astype(F32).T.astype(BF)

    def block(b):
        q = qh[b]
        top = jnp.full((8, ROWS), -3e38, F32)
        for c in range(0, SRC_ALL, 128):
            s = nt(kh[c : c + 128, :], q) + bias[c : c + 128, :]
            sbuf[c : c + 128, :] = s
            top = jnp.maximum(top, fold8(s, jnp.max))
        top = jnp.max(top, axis=0, keepdims=True)
        total = jnp.zeros((8, ROWS), F32)
        for c in range(0, SRC_ALL, 128):
            p = jnp.exp2((sbuf[c : c + 128, :] - top) * EXP2_SCALE)
            total = total + fold8(p, jnp.sum)
            pbuf[c : c + 128, :] = p.astype(BF)
        inv = 1.0 / jnp.sum(total, axis=0, keepdims=True)
        oT = nn(vT[...], pbuf[...]) * inv
        oT_out[b] = oT.astype(BF)
        stat_out[b] = jnp.concatenate([jnp.broadcast_to(top, (8, ROWS)), jnp.broadcast_to(inv, (8, ROWS))], axis=0)
        att_send[b] = oT.T.astype(BF)

    block(src)
    att_in[src] = att_send[src]

    def later(k):
        q_swap.arrive(k)
        b = src_step(src, k, True)
        block(b)
        back = src_step(0, k, True)
        a_swap.send(back)

    each(N_SRC, later)
    qh_out[...] = qh[...]
    kh_out[...] = kh[...]
    vh_out[...] = vh[...]
    a_swap.arrive_all()
    for h in range(N_SRC):
        att_out[:, h * HEAD : (h + 1) * HEAD] = att_in[h]
    k_swap.sent_all()
    v_swap.sent_all()
    q_swap.sent_all()
    a_swap.sent_all()


def gelu_pair(x):
    k = jnp.tanh(GELU_SCALE * (x + CUBIC_TERM * x * x * x))
    value = 0.5 * x * (1.0 + k)
    slope = 0.5 * (1.0 + k) + 0.5 * x * (1.0 - k * k) * GELU_SCALE * (1.0 + 3.0 * CUBIC_TERM * x * x)
    return value, slope


def iota(shape, dim):
    return lax.broadcasted_iota(jnp.int32, shape, dim)


def expert_kernel(
    att, hid, dout, w_out, gain, router, ids, slots, f_in, f_out,
    dhid, og, d_fin, d_fout, r_part, g_part,
    mixed, xin, hit_f, hitT, xs, gs, ms, xr, gr, mr, xall, gall, mall,
    actg, dpT, dpr, part, pr, gps, gpr, ps, br, gsum, gb,
    x_sem, g_sem, m_sem, xa_sem, ga_sem, ma_sem, p_sem, gp_sem, b_sem, gb_sem,
):
    src, tok = lax.axis_index("src"), lax.axis_index("tok")
    greet(src, tok)
    x_swap = Swap("tok", tok, x_sem, lambda p: xs.at[rows(p, 16)], lambda i: xr.at[rows(i, 16)])
    g_swap = Swap("tok", tok, g_sem, lambda p: gs.at[rows(p, 16)], lambda i: gr.at[rows(i, 16)])
    m_swap = Swap("tok", tok, m_sem, lambda p: ms.at[rows(p, 8)], lambda i: mr.at[rows(i, 8)])
    xa_swap = Swap("src", src, xa_sem, lambda p: xall.at[rows(src, 64)], lambda i: xall.at[rows(i, 64)])
    ga_swap = Swap("src", src, ga_sem, lambda p: gall.at[rows(src, 64)], lambda i: gall.at[rows(i, 64)])
    ma_swap = Swap("src", src, ma_sem, lambda p: mall.at[src], lambda i: mall.at[i])
    p_swap = Swap("src", src, p_sem, lambda p: part.at[rows(p, 64)], lambda i: pr.at[i])
    gp_swap = Swap("src", src, gp_sem, lambda p: gps.at[p // 2], lambda i: gpr.at[i])
    b_swap = Swap("tok", tok, b_sem, lambda p: ps.at[rows(p, 16)], lambda i: br.at[rows(i, 16)])
    gb_swap = Swap("tok", tok, gb_sem, lambda p: gsum, lambda i: gb.at[rows(i, 8)])

    id1, id2 = ids[:, 0:1], ids[:, 1:2]
    slot1, slot2 = slots[:, 0:1], slots[:, 1:2]
    live1 = (id1 < N_TOK) & (slot1 >= 0)
    live2 = (id2 < N_TOK) & (slot2 >= 0)
    aim1 = jnp.where(live1, id1 * CAP + slot1, -1)
    aim2 = jnp.where(live2, id2 * CAP + slot2, -1)
    j = iota((ROWS, ROWS), 1)
    key = (j // 16) * CAP + j % CAP
    hit = jnp.where((aim1 == key) | (aim2 == key), 1.0, 0.0)
    hit_f[...] = hit.astype(BF)
    hitT[...] = hit.T.astype(BF)
    row_blk = (iota((ROWS, ROWS), 0) // CAP) % 4
    col_blk = (j // CAP) % 4
    zero = jnp.zeros((ROWS, ROWS), BF)

    def to_experts(ref, out):
        acc = None
        for b in range(4):
            term = nn(jnp.where(row_blk == b, hitT[...], zero), ref[:, b * 256 : (b + 1) * 256])
            acc = term if acc is None else acc + term
        out[...] = acc.astype(BF)

    to_experts(dout, gs)
    g_swap.send_all()
    gr[rows(tok, 16), :] = gs[rows(tok, 16), :]

    mixed[...] = hid[...].astype(F32) + nn(att[...], w_out[...])
    inv_parts = []
    for r in range(0, ROWS, 64):
        m = mixed[r : r + 64, :]
        centred = m - jnp.mean(m, axis=1, keepdims=True)
        inv = lax.rsqrt(jnp.mean(centred * centred, axis=1, keepdims=True) + NORM_EPS)
        inv_parts.append(inv)
        normed = centred * inv
        mixed[r : r + 64, :] = normed
        xin[r : r + 64, :] = (normed * gain[...]).astype(BF)
    inv_std = jnp.concatenate(inv_parts, axis=0)
    logits = nn(xin[...], router[...])
    lane = iota((ROWS, HEAD), 1)
    pick1 = jnp.where(id1 == lane, 1.0, 0.0)
    pick2 = jnp.where(id2 == lane, 1.0, 0.0)
    gap = jnp.sum(logits * (pick1 - pick2), axis=1, keepdims=True)
    gate1 = 1.0 / (1.0 + jnp.exp(-gap))
    gate2 = 1.0 / (1.0 + jnp.exp(gap))
    low1 = gate1.astype(BF).astype(F32)
    low2 = gate2.astype(BF).astype(F32)

    to_experts(xin, xs)
    x_swap.send_all()
    xr[rows(tok, 16), :] = xs[rows(tok, 16), :]
    base = (src % 2) * 64 + tok * CAP
    own1 = jnp.where(live1 & (id1 == lane // 8), 1.0, 0.0)
    own2 = jnp.where(live2 & (id2 == lane // 8), 1.0, 0.0)
    at1 = jnp.where(lane == base + slot1, 1.0, 0.0)
    at2 = jnp.where(lane == base + slot2, 1.0, 0.0)
    ms[...] = nn((own1 * low1).T.astype(BF), at1.astype(BF)) + nn((own2 * low2).T.astype(BF), at2.astype(BF))
    m_swap.send_all()
    mr[rows(tok, 8), :] = ms[rows(tok, 8), :]

    i64, j256 = iota((64, ROWS), 0), iota((64, ROWS), 1)
    take = [jnp.where(j256 == (i64 // CAP) * 16 + b * CAP + i64 % CAP, 1.0, 0.0).astype(BF) for b in range(4)]

    def unpack(got, out):
        for b in range(4):
            out[rows(src, 64), b * 256 : (b + 1) * 256] = nn(take[b], got[...]).astype(BF)

    g_swap.arrive_all()
    unpack(gr, gall)
    ga_swap.send_all()
    x_swap.arrive_all()
    unpack(xr, xall)
    xa_swap.send_all()
    m_swap.arrive_all()
    mall[src] = fold8(mr[...], jnp.sum)
    ma_swap.send_all()
    ga_swap.arrive_all()
    xa_swap.arrive_all()
    ma_swap.arrive_all()
    gate_row = jnp.concatenate([mall[2 * i][0:1, :] + mall[2 * i + 1][0:1, :] for i in range(4)], axis=1)

    gate_acc = jnp.zeros((8, 512), F32)
    for c in range(0, 512, 128):
        pre = nt(f_in[c : c + 128, :], xall[...])
        value, slope = gelu_pair(pre)
        act = value.astype(BF).astype(F32)
        back = nt(f_out[c : c + 128, :], gall[...])
        gate_acc = gate_acc + fold8(back * act, jnp.sum)
        actg[c : c + 128, :] = (act * gate_row).astype(BF)
        dp = gate_row * back * slope
        dpT[c : c + 128, :] = dp.astype(BF)
        dpr[:, c : c + 128] = dp.T.astype(BF)
    gate_tot = jnp.sum(gate_acc, axis=0, keepdims=True)
    for i in range(4):
        gps[i] = jnp.broadcast_to(gate_tot[:, i * HEAD : (i + 1) * HEAD], (8, HEAD))
    gp_swap.send_all()
    for r in range(0, 512, 256):
        part[r : r + 256, :] = nn(dpr[r : r + 256, :], f_in[...]).astype(BF)
    p_swap.send_all()
    pr[src] = part[rows(src, 64), :]
    gpr[src] = gps[src // 2]
    for c in range(0, 512, 128):
        d_fin[c : c + 128, :] = nn(dpT[c : c + 128, :], xall[...]).astype(BF)
        d_fout[c : c + 128, :] = nn(actg[c : c + 128, :], gall[...]).astype(BF)
    p_swap.arrive_all()
    gp_swap.arrive_all()
    gsum[...] = jnp.sum(gpr[...], axis=0)
    gb_swap.send_all()
    gb[rows(tok, 8), :] = gsum[...]
    acc = None
    for b in range(4):
        blk = jnp.sum(pr[:, :, b * 256 : (b + 1) * 256].astype(F32), axis=0).astype(BF)
        term = nn(take[b].astype(F32).T.astype(BF), blk)
        acc = term if acc is None else acc + term
    ps[...] = acc.astype(BF)
    b_swap.send_all()
    br[rows(tok, 16), :] = ps[rows(tok, 16), :]

    gb_swap.arrive_all()
    first = jnp.where(lane % 8 == 0, 1.0, 0.0)
    got1 = nn(own1 * first, gb[...], precision=lax.Precision.HIGHEST)
    got2 = nn(own2 * first, gb[...], precision=lax.Precision.HIGHEST)
    grad1 = jnp.sum(got1 * at1, axis=1, keepdims=True)
    grad2 = jnp.sum(got2 * at2, axis=1, keepdims=True)
    logit_grad = gate1 * gate2 * (grad1 - grad2)
    column = (pick1 - pick2) * logit_grad
    col_hi = column.astype(BF)
    col_lo = (column - col_hi.astype(F32)).astype(BF)
    colT = column.T
    colT_hi = colT.astype(BF)
    colT_lo = (colT - colT_hi.astype(F32)).astype(BF)
    r_part[...] = (nn(colT_hi, xin[...]) + nn(colT_lo, xin[...])).T
    b_swap.arrive_all()
    gain_rows = []
    scaled_sum = jnp.zeros((ROWS, 1), F32)
    cross_sum = jnp.zeros((ROWS, 1), F32)
    scaled_all = []
    for b in range(4):
        cut = slice(b * 256, (b + 1) * 256)
        total = nn(jnp.where(col_blk == b, hit_f[...], zero), br[...])
        total = total + nt(col_hi, router[cut, :]) + nt(col_lo, router[cut, :])
        normed = mixed[:, cut]
        row = jnp.sum(total * normed, axis=0, keepdims=True)
        gain_rows += [row[:, :HEAD], row[:, HEAD:]]
        scaled = total * gain[:, cut]
        scaled_all.append(scaled)
        scaled_sum = scaled_sum + jnp.sum(scaled, axis=1, keepdims=True)
        cross_sum = cross_sum + jnp.sum(scaled * normed, axis=1, keepdims=True)
    g_part[...] = jnp.concatenate(gain_rows, axis=0)
    mean1 = scaled_sum * (1.0 / WIDTH)
    mean2 = cross_sum * (1.0 / WIDTH)
    for b in range(4):
        cut = slice(b * 256, (b + 1) * 256)
        dhid[:, cut] = (
            dout[:, cut].astype(F32) + inv_std * (scaled_all[b] - mean1 - mixed[:, cut] * mean2)
        ).astype(BF)
    for h in range(N_SRC):
        og[h] = nt(dhid[...], w_out[h * HEAD : (h + 1) * HEAD, :]).astype(BF)
    for swap in (x_swap, g_swap, m_swap, xa_swap, ga_swap, ma_swap, p_swap, gp_swap, b_swap, gb_swap):
        swap.sent_all()


def backward_kernel(
    og, qh, kh, vh, oT, stat, len_ref, att, dhid, r_part, g_part,
    dq, dk, dv, dw, d_router, d_gain,
    ogr, dqs, dqr, dka, dva, dks, dvs, dkr, dvr, kT, bias, pbuf, dsbuf,
    w1, c1, w2, yr, w3, sr, x4, xr, rg, rsend, ra, gr, gt, gmid,
    og_sem, dq_sem, dk_sem, dv_sem, c_sem, y_sem, s_sem, xh_sem, rg_sem, ra_sem, gr_sem, gt_sem,
):
    src, tok = lax.axis_index("src"), lax.axis_index("tok")
    greet(src, tok)
    y_me, x_me, c_me = tok // 4, (tok // 2) % 2, tok % 2
    og_swap = Swap("src", src, og_sem, lambda p: og.at[p], lambda i: ogr.at[i])
    dq_swap = Swap("src", src, dq_sem, lambda p: dqs.at[p], lambda i: dqr.at[i])
    dk_swap = Swap("src", src, dk_sem, lambda p: dks.at[rows(p, 128)], lambda i: dkr.at[i])
    dv_swap = Swap("src", src, dv_sem, lambda p: dvs.at[rows(p, 128)], lambda i: dvr.at[i])
    s_swap = Swap("src", src, s_sem, lambda p: w3.at[p], lambda i: sr.at[i])
    rg_swap = Swap("src", src, rg_sem, lambda p: rg.at[src], lambda i: rg.at[i])
    ra_swap = Swap("tok", tok, ra_sem, lambda p: rsend, lambda i: ra.at[i])
    gr_swap = Swap("src", src, gr_sem, lambda p: g_part, lambda i: gr.at[i])
    gt_swap = Swap("tok", tok, gt_sem, lambda p: gmid, lambda i: gt.at[i])
    og_swap.send_all()
    gr_swap.send_all()
    gr[src] = g_part[...]
    ogr[src] = og[src]

    for i in range(8):
        cut = slice(i * HEAD, (i + 1) * HEAD)
        attT = att[:, cut].astype(F32).T.astype(BF)
        w = nn(attT, dhid[...]).astype(BF)
        w1[i, 0, :, :WIDTH] = w[:64]
        w1[i, 1, :, :WIDTH] = w[64:]
        r = r_part[cut, :].astype(BF)
        w1[i, 0, :, WIDTH:] = r[:64]
        w1[i, 1, :, WIDTH:] = r[64:]
    core_copy = remote(w1.at[:, 1 - c_me], c1, c_sem.at[0], c_sem.at[1], "tok", tok_step(tok, 1))
    core_copy.start()

    kT[...] = kh[...].astype(F32).T.astype(BF)
    fill_bias(len_ref[tok], bias)
    dka[...] = jnp.zeros_like(dka)
    dva[...] = jnp.zeros_like(dva)

    def block(b):
        q, d_o = qh[b], ogr[b]
        row_term = jnp.sum(d_o.astype(F32).T * oT[b].astype(F32), axis=0, keepdims=True)
        top, inv = stat[b][0:1, :], stat[b][8:9, :]
        for c in range(0, SRC_ALL, 128):
            s = nt(kh[c : c + 128, :], q) + bias[c : c + 128, :]
            p = jnp.exp2((s - top) * EXP2_SCALE) * inv
            pbuf[c : c + 128, :] = p.astype(BF)
            dp = nt(vh[c : c + 128, :], d_o)
            dsbuf[c : c + 128, :] = (p * (dp - row_term) * FACTOR).astype(BF)
        dqs[b] = nn(kT[...], dsbuf[...]).T.astype(BF)
        dka[...] += nn(dsbuf[...], q)
        dva[...] += nn(pbuf[...], d_o)

    def turn(k):
        og_swap.arrive(k)
        block(src_step(src, k, True))
        dq_swap.send(src_step(0, k, True))

    block(src)
    dqr[src] = dqs[src]

    core_copy.wait_recv()
    for i in range(8):
        w2[i] = (w1[i, c_me].astype(F32) + c1[i].astype(F32)).astype(BF)

    def y_copy(k, to, slot):
        return remote(w2.at[pl.ds((to // 4) * 2, 2)], yr.at[slot // 4], y_sem.at[0, k], y_sem.at[1, k], "tok", to)

    each(4, lambda k: y_copy(k, tok_step(tok, 4 * k), tok).start())
    yr[y_me] = w2[pl.ds(y_me * 2, 2)]
    for k in (1, 2, 3):
        turn(k)
    gr_swap.arrive_all()
    gmid[...] = jnp.sum(gr[...], axis=0)
    gt_swap.send_all()
    gt[tok] = gmid[...]

    def y_done(k):
        sender = tok_step(tok, 4 * k, True)
        y_copy(k, sender, sender).wait_recv()

    each(4, y_done)
    for x in range(2):
        sums = jnp.sum(yr[:, x].astype(F32), axis=0)
        x4[x] = sums
    for i in range(8):
        w3[i] = jnp.concatenate([x4[0, i * 8 : (i + 1) * 8, :], x4[1, i * 8 : (i + 1) * 8, :]], axis=0).astype(BF)
    s_swap.send_all()
    sr[src] = w3[src]
    for k in (4, 5):
        turn(k)
    s_swap.arrive_all()
    sums = jnp.sum(sr[...].astype(F32), axis=0)
    xr[0] = sums[:8]
    xr[1] = sums[8:]
    x_copy = remote(xr.at[1 - x_me], xr.at[2], xh_sem.at[0], xh_sem.at[1], "tok", tok_step(tok, 2))
    x_copy.start()
    for k in (6, 7):
        turn(k)
    dks[...] = dka[...].astype(BF)
    dk_swap.send_all()
    dvs[...] = dva[...].astype(BF)
    dv_swap.send_all()
    dkr[src] = dks[rows(src, 128), :]
    dvr[src] = dvs[rows(src, 128), :]
    x_copy.wait_recv()
    mine = xr[x_me] + xr[2]
    dw[...] = mine[:, :WIDTH]
    rg[src] = mine[:, WIDTH:]
    rg_swap.send_all()
    rg_swap.arrive_all()
    for i in range(0, 8, 2):
        rsend[i * 8 : i * 8 + 16, :] = jnp.concatenate([rg[i], rg[i + 1]], axis=0).astype(BF)
    ra_swap.send_all()
    ra[tok] = rsend[...]
    gt_swap.arrive_all()
    d_gain[...] = jnp.sum(gt[...], axis=0)
    dq_swap.arrive_all()
    for h in range(N_SRC):
        dq[:, h * HEAD : (h + 1) * HEAD] = dqr[h]
    dk_swap.arrive_all()
    dv_swap.arrive_all()
    for h in range(N_SRC):
        dk[:, h * HEAD : (h + 1) * HEAD] = dkr[h]
        dv[:, h * HEAD : (h + 1) * HEAD] = dvr[h]
    ra_swap.arrive_all()
    for t in range(N_TOK):
        d_router[t * 64 : (t + 1) * 64, :] = ra[t].astype(F32)
    for swap in (og_swap, dq_swap, dk_swap, dv_swap, s_swap, rg_swap, ra_swap, gr_swap, gt_swap):
        swap.sent_all()
    core_copy.wait_send()
    x_copy.wait_send()
    each(4, lambda k: y_copy(k, tok_step(tok, 4 * k), tok).wait_send())


VMEM = pl.BlockSpec(memory_space=pltpu.VMEM)
SMEM = pl.BlockSpec(memory_space=pltpu.SMEM)


def call(kernel, in_specs, outs, scratch, collective_id, args):
    return pl.pallas_call(
        kernel,
        out_shape=tuple(jax.ShapeDtypeStruct(s, d) for s, d in outs),
        in_specs=in_specs,
        out_specs=tuple(VMEM for _ in outs),
        scratch_shapes=scratch,
        compiler_params=pltpu.CompilerParams(
            collective_id=collective_id, has_side_effects=True, vmem_limit_bytes=58 * 1024 * 1024
        ),
    )(*args)


def vm(*shape, dtype=BF):
    return pltpu.VMEM(shape, dtype)


def sems(*shape):
    return pltpu.SemaphoreType.DMA(shape)


def on_device(
    hidden_in, d_out, queries, keys, values, source_len, out_weight, norm_gain, router,
    expert_ids, expert_slots, fc_in, fc_out,
):
    att, qh, kh, vh, oT, stat = call(
        attend_kernel,
        [VMEM, VMEM, VMEM, SMEM],
        [
            ((ROWS, WIDTH), BF), ((8, ROWS, HEAD), BF), ((SRC_ALL, HEAD), BF), ((SRC_ALL, HEAD), BF),
            ((8, HEAD, ROWS), BF), ((8, 16, ROWS), F32),
        ],
        [
            vm(8, ROWS, HEAD), vm(SRC_ALL, HEAD), vm(SRC_ALL, HEAD), vm(8, ROWS, HEAD), vm(8, ROWS, HEAD),
            vm(HEAD, SRC_ALL), vm(SRC_ALL, ROWS, dtype=F32), vm(SRC_ALL, ROWS), vm(SRC_ALL, ROWS, dtype=F32),
        ] + [sems(2, 8)] * 4,
        1,
        (queries, keys[0], values[0], source_len),
    )
    dhid, og, d_fin, d_fout, r_part, g_part = call(
        expert_kernel,
        [VMEM] * 10,
        [
            ((ROWS, WIDTH), BF), ((8, ROWS, HEAD), BF), ((512, WIDTH), BF), ((512, WIDTH), BF),
            ((WIDTH, HEAD), F32), ((8, HEAD), F32),
        ],
        [
            vm(ROWS, WIDTH, dtype=F32), vm(ROWS, WIDTH), vm(ROWS, ROWS), vm(ROWS, ROWS),
            vm(ROWS, ROWS), vm(ROWS, ROWS), vm(HEAD, HEAD, dtype=F32),
            vm(ROWS, ROWS), vm(ROWS, ROWS), vm(HEAD, HEAD, dtype=F32),
            vm(512, WIDTH), vm(512, WIDTH), vm(8, 8, HEAD, dtype=F32),
            vm(512, 512), vm(512, 512), vm(512, 512), vm(512, WIDTH), vm(8, 64, WIDTH),
            vm(4, 8, HEAD, dtype=F32), vm(8, 8, HEAD, dtype=F32),
            vm(ROWS, ROWS), vm(ROWS, ROWS), vm(8, HEAD, dtype=F32), vm(HEAD, HEAD, dtype=F32),
        ] + [sems(2, 16)] * 3 + [sems(2, 8)] * 5 + [sems(2, 16)] * 2,
        2,
        (att, hidden_in, d_out, out_weight, norm_gain[None], router, expert_ids, expert_slots, fc_in[0], fc_out[0]),
    )
    wide = WIDTH + HEAD
    dq, dk, dv, dw, d_router, d_gain = call(
        backward_kernel,
        [VMEM] * 6 + [SMEM] + [VMEM] * 4,
        [
            ((ROWS, WIDTH), BF), ((HEAD, WIDTH), BF), ((HEAD, WIDTH), BF), ((8, WIDTH), F32),
            ((WIDTH, HEAD), F32), ((8, HEAD), F32),
        ],
        [
            vm(8, ROWS, HEAD), vm(8, ROWS, HEAD), vm(8, ROWS, HEAD),
            vm(SRC_ALL, HEAD, dtype=F32), vm(SRC_ALL, HEAD, dtype=F32), vm(SRC_ALL, HEAD), vm(SRC_ALL, HEAD),
            vm(8, HEAD, HEAD), vm(8, HEAD, HEAD), vm(HEAD, SRC_ALL), vm(SRC_ALL, ROWS, dtype=F32),
            vm(SRC_ALL, ROWS), vm(SRC_ALL, ROWS),
            vm(8, 2, 64, wide), vm(8, 64, wide), vm(8, 64, wide), vm(4, 2, 64, wide), vm(8, 16, wide),
            vm(8, 16, wide), vm(2, 64, wide, dtype=F32), vm(3, 8, wide, dtype=F32),
            vm(8, 8, HEAD, dtype=F32), vm(64, HEAD), vm(16, 64, HEAD), vm(8, 8, HEAD, dtype=F32),
            vm(16, 8, HEAD, dtype=F32), vm(8, HEAD, dtype=F32),
        ] + [sems(2, 8)] * 4 + [sems(2), sems(2, 4), sems(2, 8), sems(2), sems(2, 8), sems(2, 16), sems(2, 8), sems(2, 16)],
        3,
        (og, qh, kh, vh, oT, stat, source_len, att, dhid, r_part, g_part),
    )
    return (
        dhid, dq, dk[None], dv[None], dw, d_router, d_gain.reshape(-1), d_fin[None], d_fout[None],
    )


def solution(mesh):
    return jax.shard_map(
        on_device,
        mesh=mesh,
        in_specs=(
            P(("tok", "src"), None), P(("tok", "src"), None), P(("tok", "src"), None),
            P("tok", "src", None), P("tok", "src", None), P(), P(), P(), P(),
            P(("tok", "src"), None), P(("tok", "src"), None), P("tok", "src", None), P("tok", "src", None),
        ),
        out_specs=(
            P(("tok", "src"), None), P(("tok", "src"), None), P("tok", "src", None), P("tok", "src", None),
            P(("tok", "src"), None), P(), P(), P("tok", "src", None), P("tok", "src", None),
        ),
        check_vma=False,
    )
```

time: 1240 us -> 170 us (0.14)
  waiting for transfers between devices: 995 us -> 0 us
  Pallas kernels: 0 us -> 157 us
  blocking collectives: 104 us -> 0 us
  matrix products: 57.7 us -> 0 us
  local copies, waits for them, and re-layouts: 34.6 us -> 11 us
  starting transfers between devices: 17.1 us -> 0 us
  between operations: 15.2 us -> 0.74 us
  other arithmetic: 14.4 us -> 0 us
    reduce_scatter x4 -> x0, waiting for transfers between devices: 775 us -> none  [the longest x1 647 us: on_device(): lax.psum_scatter(jnp.einsum('th,td->hd', attended, d_hidden, preferred_el...]
    pallas_call x0 -> x3, Pallas kernels: none -> 157 us  [call(): pl.pallas_call(kernel, out_shape=tuple((jax.ShapeDtypeStruct(s, d) for s,...]
    all_gather x4 -> x0, waiting for transfers between devices: 134 us -> none  [the longest x1 43.9 us: on_device(): lax.all_gather(keys[0], 'src', axis=0, tiled=True)]
    psum x1 -> x0, blocking collectives: 62.7 us -> none  [on_device(): d_router, d_gain = lax.psum((router_part, gain_part), ('tok', 'src'))]
    dot_general x21 -> x0, matrix products: 49.6 us -> none  [the longest x1 6.24 us: on_device(): jnp.einsum('thd,shd->hts', out_heads, value_all, preferred_element_type=j...]
    unnamed x11 -> x0, waiting for transfers between devices: 36.9 us -> none
    psum x1 -> x0, waiting for transfers between devices: 30.5 us -> none  [on_device(): d_router, d_gain = lax.psum((router_part, gain_part), ('tok', 'src'))]
    all_to_all x2 -> x0, blocking collectives: 25.3 us -> none  [the longest x1 14.5 us: on_device(): lax.all_to_all(sent_in, 'tok', split_axis=0, concat_axis=1, tiled=True)]
  transfers between devices with their start and end apart: 13 -> 0, of which waited for: 13 -> 0; matrix products, arithmetic and copies ran while one was open for 6% -> 0% of each run, Pallas kernels for 0% -> 0%
where the time goes in v1:
time: 170 us; the launch traced here: 169 us
  Pallas kernels  157 us (92%)
  local copies, waits for them, and re-layouts  11 us (6%)
    pallas_call x3, Pallas kernels, call(): pl.pallas_call(kernel, out_shape=tuple((jax.ShapeDtypeStruct(s, d) for s,...  157 us
    unnamed x27, local copies, waits for them, and re-layouts  11 us

profile of v1, /device:TPU:0, one launch (start us, length us, event | category | flops | bytes accessed | tf_op | source)
XLA Modules:
  0.0 168.7 jit_solution(15276678386087246503)
XLA Ops:
  0.6 1.5 copy.22.ids
  2.1 1.5 copy.23.slots
  3.6 30.0 %shard_map.196 = (bf16[256,1024]{1,0:T(8,128)(2,1)}, bf16[8,256,128]{2,1,0:T(8,128)(2,1)}, bf16[1024,128]{1,0:T(8,128)(2,1)}, bf16[1024,128]{1,0:T(8,128)(2,1)},...) custom-call(bf16[256,1024]{1,0:T(8,128)(2,1)} %q_ref.1, bf16[128,1024]{1,0:T(8,128)(2,1)} %bitcast.16, ...), custom_call_target="tpu_custom_call" | custom-call | tf_op jit(solution)/shard_map/pallas_call | solution.py:521
  33.6 73.8 %shard_map.197 = (bf16[256,1024]{1,0:T(8,128)(2,1)}, bf16[8,256,128]{2,1,0:T(8,128)(2,1)}, bf16[512,1024]{1,0:T(8,128)(2,1)}, bf16[512,1024]{1,0:T(8,128)(2,1)}, f32[1024,128]{1,0:T(8,128)}, /*index=5*/f32[8,128]{1,0:T(8,128)}) custom-call(bf16[256,1024]{1,0:T(8,128)(2,1)} %get-tuple-element.27.att, bf16[256,1024]{1,0:T(8,128)(2,1)} %hid.1, ...), custom_call_target="tpu_custom_call" | custom-call | tf_op jit(solution)/shard_map/pallas_call | solution.py:521
  107.4 0.0 copy-start
  107.4 53.2 %shard_map.198 = (bf16[256,1024]{1,0:T(8,128)(2,1)}, bf16[128,1024]{1,0:T(8,128)(2,1)}, bf16[128,1024]{1,0:T(8,128)(2,1)}, f32[8,1024]{1,0:T(8,128)}, f32[1024,128]{1,0:T(8,128)}, /*index=5*/f32[8,128]{1,0:T(8,128)}) custom-call(bf16[8,256,128]{2,1,0:T(8,128)(2,1)} %get-tuple-element.29.og, bf16[8,256,128]{2,1,0:T(8,128)(2,1)} %get-tuple-element.30.qh, ...), custom_call_target="tpu_custom_call" | custom-call | tf_op jit(solution)/shard_map/pallas_call | solution.py:521
  160.6 0.0 copy-start.5
  160.6 0.0 copy-start.4
  160.7 0.0 copy-start.6
  160.7 0.0 copy-start.3
  160.7 0.0 copy-done
  160.7 0.0 copy-start.7
  160.7 0.8 copy.33
  161.5 1.9 %copy.34 = bf16[256,1024]{1,0:T(8,128)(2,1)} copy(bf16[256,1024]{1,0:T(8,128)(2,1)} %get-tuple-element.55) | data formatting | bytes 1048576
  163.4 0.7 copy.35
  164.1 0.0 copy-done.4
  164.1 0.7 copy.36
  164.8 0.6 copy.37
  165.4 0.8 copy.38
  166.2 0.0 copy-done.7
  166.2 0.6 copy.39
  166.8 1.0 copy.40
  167.8 0.0 copy-done.1
  167.8 1.0 copy.41
  (6 shorter events, 0.0 us)
Async XLA Ops:
  107.4 53.2 %copy-start = (bf16[256,1024]{1,0:T(8,128)(2,1)S(1)}, bf16[256,1024]{1,0:T(8,128)(2,1)}, u32[]{:S(2)}) copy-start(bf16[256,1024]{1,0:T(8,128)(2,1)} %get-tuple-element.54.dhid) | copy-start | bytes 1572868
  160.6 2.7 %copy-start.5 = (bf16[128,1024]{1,0:T(8,128)(2,1)S(1)}, bf16[128,1024]{1,0:T(8,128)(2,1)}, u32[]{:S(2)}) copy-start(bf16[128,1024]{1,0:T(8,128)(2,1)} %get-tuple-element.38) | copy-start | bytes 786436
  160.6 3.4 %copy-start.4 = (bf16[128,1024]{1,0:T(8,128)(2,1)S(1)}, bf16[128,1024]{1,0:T(8,128)(2,1)}, u32[]{:S(2)}) copy-start(bf16[128,1024]{1,0:T(8,128)(2,1)} %get-tuple-element.39) | copy-start | bytes 786436
  160.7 4.1 %copy-start.6 = (f32[8,1024]{1,0:T(8,128)S(1)}, f32[8,1024]{1,0:T(8,128)}, u32[]{:S(2)}) copy-start(f32[8,1024]{1,0:T(8,128)} %get-tuple-element.58) | copy-start | bytes 98308
  160.7 4.7 %copy-start.3 = (f32[1024,128]{1,0:T(8,128)S(1)}, f32[1024,128]{1,0:T(8,128)}, u32[]{:S(2)}) copy-start(f32[1024,128]{1,0:T(8,128)} %get-tuple-element.59) | copy-start | bytes 1572868
  160.7 5.5 %copy-start.7 = (f32[8,128]{1,0:T(8,128)S(1)}, f32[8,128]{1,0:T(8,128)}, u32[]{:S(2)}) copy-start(f32[8,128]{1,0:T(8,128)} %get-tuple-element.42) | copy-start | bytes 12292
  160.7 6.1 %copy-start.2 = (bf16[512,1024]{1,0:T(8,128)(2,1)S(1)}, bf16[512,1024]{1,0:T(8,128)(2,1)}, u32[]{:S(2)}) copy-start(bf16[512,1024]{1,0:T(8,128)(2,1)} %get-tuple-element.43) | copy-start | bytes 3145732
  163.4 4.4 %copy-start.1 = (bf16[512,1024]{1,0:T(8,128)(2,1)S(1)}, bf16[512,1024]{1,0:T(8,128)(2,1)}, u32[]{:S(2)}) copy-start(bf16[512,1024]{1,0:T(8,128)(2,1)} %get-tuple-element.44) | copy-start | bytes 3145732

commit v2 on v0

v2 whole, which is shorter than its diff:
```python
import math

import jax
import jax.numpy as jnp
from jax import lax
from jax.experimental import pallas as pl
from jax.experimental.pallas import tpu as pltpu
from jax.sharding import PartitionSpec as P

MESH = pl.DeviceIdType.MESH
BF, F32 = jnp.bfloat16, jnp.float32
HEAD = 128
CAP = 4
NORM_EPS = 1e-05
GELU_SCALE = 0.7978845608028654
CUBIC_TERM = 0.044715
FACTOR = 1.0 / math.sqrt(HEAD)
EXP2_SCALE = FACTOR / math.log(2.0)
MASKED = -1e30
N_SRC, N_TOK = 8, 16
ROWS, WIDTH, SRC_ALL = 256, 1024, 1024


def nn(a, b, **kw):
    return lax.dot_general(a, b, (((1,), (0,)), ((), ())), preferred_element_type=F32, **kw)


def nt(a, b, **kw):
    return lax.dot_general(a, b, (((1,), (1,)), ((), ())), preferred_element_type=F32, **kw)


def src_step(src, k, back=False):
    x, z = src // 4, src % 4
    z = (z + 4 - k % 4) % 4 if back else (z + k % 4) % 4
    return ((x + k // 4) % 2) * 4 + z


def tok_step(tok, k, back=False):
    y, x, c = tok // 4, (tok // 2) % 2, tok % 2
    y = (y + 4 - k // 4) % 4 if back else (y + k // 4) % 4
    return y * 4 + ((x + (k // 2) % 2) % 2) * 2 + (c + k % 2) % 2


def remote(src_ref, dst_ref, send_sem, recv_sem, axis, peer):
    return pltpu.make_async_remote_copy(
        src_ref=src_ref,
        dst_ref=dst_ref,
        send_sem=send_sem,
        recv_sem=recv_sem,
        device_id={axis: peer},
        device_id_type=MESH,
    )


def each(count, body, low=1):
    def step(k, carry):
        body(k)
        return carry

    lax.fori_loop(low, count, step, 0)


def greet(src, tok):
    bar = pltpu.get_barrier_semaphore()
    waits = 0
    if src is not None:
        waits += N_SRC - 1
        each(N_SRC, lambda k: pl.semaphore_signal(bar, inc=1, device_id={"src": src_step(src, k)}, device_id_type=MESH))
    if tok is not None:
        waits += N_TOK - 1
        each(N_TOK, lambda k: pl.semaphore_signal(bar, inc=1, device_id={"tok": tok_step(tok, k)}, device_id_type=MESH))
    pl.semaphore_wait(bar, waits)


class Swap:
    def __init__(self, axis, me, sems, source, target, blocks, low=1, high=None):
        self.axis, self.me, self.sems = axis, me, sems
        self.source, self.target = source, target
        self.low, self.high = low, high or (N_SRC if axis == "src" else N_TOK)
        self.held = blocks(self.high - low)
        self.step = src_step if axis == "src" else tok_step

    def send(self, k):
        to = self.step(self.me, k)
        remote(self.source(to), self.target(self.me), self.sems.at[0], self.sems.at[1], self.axis, to).start()

    def send_all(self):
        each(self.high, self.send, self.low)

    def arrive_all(self):
        bulk_wait(self.held, self.sems.at[1])

    def sent_all(self):
        bulk_wait(self.held, self.sems.at[0])


def bulk_wait(ref, sem):
    pltpu.make_async_copy(ref, ref, sem).wait()


def lanes(index):
    return pl.ds(pl.multiple_of(index * HEAD, HEAD), HEAD)


def rows(index, size):
    return pl.ds(pl.multiple_of(index * size, size), size)


def fold8(value, op):
    return op(value.reshape(value.shape[0] // 8, 8, value.shape[1]), axis=0)


def gelu_pair(x):
    k = jnp.tanh(GELU_SCALE * (x + CUBIC_TERM * x * x * x))
    value = 0.5 * x * (1.0 + k)
    slope = 0.5 * (1.0 + k) + 0.5 * x * (1.0 - k * k) * GELU_SCALE * (1.0 + 3.0 * CUBIC_TERM * x * x)
    return value, slope


def iota(shape, dim):
    return lax.broadcasted_iota(jnp.int32, shape, dim)


def vm(*shape, dtype=BF):
    return pltpu.VMEM(shape, dtype)


def sems(*shape):
    return pltpu.SemaphoreType.DMA(shape)


SCRATCH = dict(
    hid=vm(ROWS, WIDTH), w_out=vm(WIDTH, WIDTH), f_in=vm(512, WIDTH), f_out=vm(512, WIDTH),
    qh=vm(8, ROWS, HEAD), kh=vm(SRC_ALL, HEAD), vh=vm(SRC_ALL, HEAD), att_in=vm(8, ROWS, HEAD),
    att_send=vm(8, ROWS, HEAD), vT=vm(HEAD + 16, SRC_ALL), kT=vm(HEAD, SRC_ALL), sbuf=vm(SRC_ALL, ROWS, dtype=F32),
    pbuf=vm(SRC_ALL, ROWS), dsbuf=vm(SRC_ALL, ROWS),
    oT=vm(8, HEAD, ROWS), stat=vm(8, 16, ROWS, dtype=F32), att=vm(ROWS, WIDTH),
    mixed=vm(ROWS, WIDTH, dtype=F32), xin=vm(ROWS, WIDTH), hitT=vm(ROWS, ROWS),
    xs=vm(ROWS, ROWS), gs=vm(ROWS, ROWS), ms=vm(HEAD, HEAD, dtype=F32),
    xr=vm(ROWS, ROWS), gr=vm(ROWS, ROWS), mr=vm(HEAD, HEAD, dtype=F32),
    xall=vm(512, WIDTH), gall=vm(512, WIDTH), mall=vm(8, 8, HEAD, dtype=F32),
    backT=vm(512, 512, dtype=F32), actg=vm(512, 512), dpT=vm(512, 512), dpr=vm(512, 512),
    part=vm(512, WIDTH), pr=vm(8, 64, WIDTH), gps=vm(4, 8, HEAD, dtype=F32), gpr=vm(8, 8, HEAD, dtype=F32),
    ps=vm(ROWS, ROWS), br=vm(ROWS, ROWS), gsum=vm(8, HEAD, dtype=F32), gb=vm(HEAD, HEAD, dtype=F32),
    dhid=vm(ROWS, WIDTH), d_fin=vm(512, WIDTH), d_fout=vm(512, WIDTH),
    og=vm(8, ROWS, HEAD), ogr=vm(8, ROWS, HEAD), dqs=vm(8, ROWS, HEAD), dqr=vm(8, ROWS, HEAD),
    dka=vm(SRC_ALL, HEAD, dtype=F32), dva=vm(SRC_ALL, HEAD, dtype=F32), dks=vm(SRC_ALL, HEAD), dvs=vm(SRC_ALL, HEAD),
    dkr=vm(8, HEAD, HEAD), dvr=vm(8, HEAD, HEAD),
    w1=vm(8, 2, 64, WIDTH), c1=vm(8, 64, WIDTH), x5=vm(3, 8, WIDTH, dtype=F32),
    wtmp=vm(8, 64, 512, dtype=F32), ya=vm(8, 64, 512), yar=vm(4, 2, 64, 512), sa=vm(8, 16, 512), sar=vm(8, 16, 512),
    sb=vm(8, 64, 512), sbr=vm(8, 64, 512), yb=vm(4, 16, 512), ybr=vm(4, 16, 512),
    r1=vm(16, 64, HEAD), r1r=vm(16, 64, HEAD), r2=vm(8, 64, HEAD), r3=vm(16, 64, HEAD),
    g1=vm(8, 8, HEAD, dtype=F32), g2=vm(16, 8, HEAD, dtype=F32),
    dw=vm(8, WIDTH, dtype=F32), d_router=vm(WIDTH, HEAD, dtype=F32), d_gain=vm(8, HEAD, dtype=F32),
    dout=vm(ROWS, WIDTH),
    k_sem=sems(2), v_sem=sems(2), qn_sem=sems(2), qf_sem=sems(2), a_sem=sems(2), x_sem=sems(2), g_sem=sems(2),
    m_sem=sems(2), xan_sem=sems(2), xaf_sem=sems(2), ga_sem=sems(2), ma_sem=sems(2), p_sem=sems(2),
    gp_sem=sems(2), b_sem=sems(2), gb_sem=sems(2), ogn_sem=sems(2), ogf_sem=sems(2), dq_sem=sems(2),
    dk_sem=sems(2), dv_sem=sems(2), c_sem=sems(2), xh_sem=sems(2), ya_sem=sems(2), yb_sem=sems(2), sa_sem=sems(2),
    sb_sem=sems(2), r1_sem=sems(2), r2_sem=sems(2), r3_sem=sems(2), g1_sem=sems(2), g2_sem=sems(2),
    io_sem=sems(17),
)
INPUTS = (
    "length", "gain", "router", "ids", "slots", "q", "k", "v", "dout_hbm", "hid_hbm", "w_out_hbm",
    "f_in_hbm", "f_out_hbm",
)
OUTPUTS = (
    "dhid_hbm", "dq_hbm", "dk_hbm", "dv_hbm", "dw_hbm", "d_router_hbm", "d_gain_hbm", "d_fin_hbm",
    "d_fout_hbm",
)


class Refs:
    pass


def block_kernel(*refs):
    R = Refs()
    for name, ref in zip(INPUTS + OUTPUTS + tuple(SCRATCH), refs, strict=True):
        setattr(R, name, ref)
    src, tok = lax.axis_index("src"), lax.axis_index("tok")
    y_me, x_me, c_me = tok // 4, (tok // 2) % 2, tok % 2
    x_lo = src // 4

    loads = [
        pltpu.make_async_copy(a, b, R.io_sem.at[i])
        for i, (a, b) in enumerate(
            (
                (R.dout_hbm, R.dout), (R.hid_hbm, R.hid), (R.w_out_hbm, R.w_out), (R.f_out_hbm, R.f_out), (R.f_in_hbm, R.f_in),
                (R.k.at[:, lanes(src)], R.kh.at[rows(src, 128)]), (R.v.at[:, lanes(src)], R.vh.at[rows(src, 128)]),
                (R.q.at[:, lanes(src)], R.qh.at[src]),
            )
        )
    ]
    for copy in loads:
        copy.start()
    greet(src, tok)

    def by_src(*way):
        return Swap("src", src, *way)

    def by_tok(*way):
        return Swap("tok", tok, *way)

    def first(ref, size=1):
        return lambda n: ref.at[pl.ds(0, n * size)]

    def at(ref):
        return lambda i: ref.at[i]

    def at_rows(ref, size):
        return lambda i: ref.at[rows(i, size)]

    k_swap = by_src(R.k_sem, lambda p: R.k.at[:, lanes(p)], at_rows(R.kh, 128), first(R.kh, 128))
    v_swap = by_src(R.v_sem, lambda p: R.v.at[:, lanes(p)], at_rows(R.vh, 128), first(R.vh, 128))
    q_way = lambda p: R.q.at[:, lanes(p)], at(R.qh), first(R.qh)
    q_near, q_far = by_src(R.qn_sem, *q_way, 1, 4), by_src(R.qf_sem, *q_way, 4, 8)
    a_swap = by_src(R.a_sem, at(R.att_send), at(R.att_in), first(R.att_in))
    x_swap = by_tok(R.x_sem, at_rows(R.xs, 16), at_rows(R.xr, 16), first(R.xr, 16))
    g_swap = by_tok(R.g_sem, at_rows(R.gs, 16), at_rows(R.gr, 16), first(R.gr, 16))
    m_swap = by_tok(R.m_sem, at_rows(R.ms, 8), at_rows(R.mr, 8), first(R.mr, 8))
    xa_way = lambda p: R.xall.at[rows(src, 64)], at_rows(R.xall, 64), first(R.xall, 64)
    xa_near, xa_far = by_src(R.xan_sem, *xa_way, 1, 4), by_src(R.xaf_sem, *xa_way, 4, 8)
    ga_swap = by_src(R.ga_sem, lambda p: R.gall.at[rows(src, 64)], at_rows(R.gall, 64), first(R.gall, 64))
    ma_swap = by_src(R.ma_sem, lambda p: R.mall.at[src], at(R.mall), first(R.mall))
    p_swap = by_src(R.p_sem, at_rows(R.part, 64), at(R.pr), first(R.pr))
    gp_swap = by_src(R.gp_sem, lambda p: R.gps.at[p // 2], at(R.gpr), first(R.gpr))
    b_swap = by_tok(R.b_sem, at_rows(R.ps, 16), at_rows(R.br, 16), first(R.br, 16))
    gb_swap = by_tok(R.gb_sem, lambda p: R.gsum, at_rows(R.gb, 8), first(R.gb, 8))
    og_way = at(R.og), at(R.ogr), first(R.ogr)
    og_near, og_far = by_src(R.ogn_sem, *og_way, 1, 4), by_src(R.ogf_sem, *og_way, 4, 8)
    dq_swap = by_src(R.dq_sem, at(R.dqs), at(R.dqr), first(R.dqr))
    dk_swap = by_src(R.dk_sem, at_rows(R.dks, 128), at(R.dkr), first(R.dkr))
    dv_swap = by_src(R.dv_sem, at_rows(R.dvs, 128), at(R.dvr), first(R.dvr))
    sa_swap = by_src(R.sa_sem, at(R.sa), at(R.sar), first(R.sar))
    sb_swap = by_src(R.sb_sem, at(R.sb), at(R.sbr), first(R.sbr))
    r1_swap = by_tok(R.r1_sem, at(R.r1), at(R.r1r), first(R.r1r))
    r2_swap = by_src(R.r2_sem, lambda p: R.r2.at[src], at(R.r2), first(R.r2))
    r3_swap = by_tok(R.r3_sem, lambda p: R.r3.at[tok], at(R.r3), first(R.r3))
    g1_swap = by_src(R.g1_sem, lambda p: R.g1.at[src], at(R.g1), first(R.g1))
    g2_swap = by_tok(R.g2_sem, lambda p: R.g2.at[tok], at(R.g2), first(R.g2))

    def y_go(sem, source, target, held):
        def send(k):
            to = tok_step(tok, 4 * k)
            remote(source(to // 4), target(y_me), sem.at[0], sem.at[1], "tok", to).start()

        each(4, send)

    def y_arrive(sem, source, target, held):
        bulk_wait(held, sem.at[1])

    def y_sent(sem, source, target, held):
        bulk_wait(held, sem.at[0])

    ya_way = (R.ya_sem, lambda y: R.ya.at[pl.ds(y * 2, 2)], at(R.yar), R.yar.at[pl.ds(0, 3)])
    yb_way = (R.yb_sem, at(R.yb), at(R.ybr), R.ybr.at[pl.ds(0, 3)])

    k_swap.send_all()
    v_swap.send_all()

    def aim_of(id_of, slot_of):
        return jnp.where((id_of < N_TOK) & (slot_of >= 0), id_of * CAP + slot_of, -1)

    j = iota((ROWS, ROWS), 0)
    key = (j // 16) * CAP + j % CAP
    aim_rows = aim_of(R.ids[...], R.slots[...])
    hitT = jnp.where((aim_rows[0:1, :] == key) | (aim_rows[1:2, :] == key), 1.0, 0.0)
    R.hitT[...] = hitT.astype(BF)
    row_blk = (j // CAP) % 4
    zero = jnp.zeros((ROWS, ROWS), BF)

    def to_experts(ref, out):
        acc = None
        for b in range(4):
            term = nn(jnp.where(row_blk == b, R.hitT[...], zero), ref[:, b * 256 : (b + 1) * 256])
            acc = term if acc is None else acc + term
        out[...] = acc.astype(BF)

    loads[0].wait()
    to_experts(R.dout, R.gs)
    g_swap.send_all()
    k_swap.sent_all()
    v_swap.sent_all()
    q_near.send_all()
    q_near.sent_all()
    q_far.send_all()
    R.gr[rows(tok, 16), :] = R.gs[rows(tok, 16), :]
    for copy in loads[5:]:
        copy.wait()
    k_swap.arrive_all()
    v_swap.arrive_all()
    length = R.length[tok]
    seen = iota((SRC_ALL, HEAD), 0) < length
    seen_row = iota((HEAD, SRC_ALL), 1) < length
    k_wide = R.kh[...].astype(F32)
    R.kh[...] = jnp.where(seen, k_wide, k_wide[0:1, :]).astype(BF)
    R.vT[:HEAD, :] = jnp.where(seen_row, R.vh[...].astype(F32).T, 0.0).astype(BF)
    R.vT[HEAD:, :] = jnp.where(seen_row[:16], 1.0, 0.0).astype(BF)

    def forward_block(b):
        q = R.qh[b]
        top = jnp.full((8, ROWS), -3e38, F32)
        for c in range(0, SRC_ALL, 128):
            s = nt(R.kh[c : c + 128, :], q)
            R.sbuf[c : c + 128, :] = s
            top = jnp.maximum(top, fold8(s, jnp.max))
        top = jnp.max(top, axis=0, keepdims=True)
        for c in range(0, SRC_ALL, 128):
            p = jnp.exp2((R.sbuf[c : c + 128, :] - top) * EXP2_SCALE)
            R.pbuf[c : c + 128, :] = p.astype(BF)
        summed = nn(R.vT[...], R.pbuf[...])
        inv = 1.0 / summed[HEAD : HEAD + 1, :]
        oT = summed[:HEAD, :] * inv
        R.oT[b] = oT.astype(BF)
        R.stat[b] = jnp.concatenate(
            [jnp.broadcast_to(top, (8, ROWS)), jnp.broadcast_to(inv, (8, ROWS))], axis=0
        )
        R.att_send[b] = oT.T.astype(BF)

    i64, j256 = iota((64, ROWS), 0), iota((64, ROWS), 1)
    take = [jnp.where(j256 == (i64 // CAP) * 16 + b * CAP + i64 % CAP, 1.0, 0.0).astype(BF) for b in range(4)]

    def unpack(got, out):
        for b in range(4):
            out[rows(src, 64), b * 256 : (b + 1) * 256] = nn(take[b], got[...]).astype(BF)

    def g_on():
        g_swap.arrive_all()
        unpack(R.gr, R.gall)
        ga_swap.send_all()

    forward_block(src)
    R.att_in[src] = R.att_send[src]

    def forward_turn(k):
        forward_block(src_step(src, k, True))
        a_swap.send(src_step(0, k, True))

    q_near.arrive_all()
    each(4, forward_turn)
    q_far.arrive_all()
    each(8, forward_turn, 4)

    id_cols = jnp.concatenate([R.ids[...], R.slots[...], R.ids[...], R.slots[...]], axis=0).astype(F32).T
    id_cols = id_cols.astype(jnp.int32)
    id1, id2, slot1, slot2 = (id_cols[:, i : i + 1] for i in range(4))
    lane = iota((ROWS, HEAD), 1)
    pick1 = jnp.where(id1 == lane, 1.0, 0.0)
    pick2 = jnp.where(id2 == lane, 1.0, 0.0)
    live1, live2 = slot1 >= 0, slot2 >= 0
    base = (src % 2) * 64 + tok * CAP
    own1 = jnp.where(live1 & (id1 < N_TOK) & (id1 == lane // 8), 1.0, 0.0)
    own2 = jnp.where(live2 & (id2 < N_TOK) & (id2 == lane // 8), 1.0, 0.0)
    at1 = jnp.where(live1 & (lane == base + slot1), 1.0, 0.0)
    at2 = jnp.where(live2 & (lane == base + slot2), 1.0, 0.0)
    for copy in loads[1:5]:
        copy.wait()
    a_swap.arrive_all()
    for h in range(N_SRC):
        R.att[:, h * HEAD : (h + 1) * HEAD] = R.att_in[h]

    R.mixed[...] = R.hid[...].astype(F32) + nn(R.att[...], R.w_out[...])
    inv_parts = []
    for r in range(0, ROWS, 64):
        m = R.mixed[r : r + 64, :]
        centred = m - jnp.mean(m, axis=1, keepdims=True)
        inv = lax.rsqrt(jnp.mean(centred * centred, axis=1, keepdims=True) + NORM_EPS)
        inv_parts.append(inv)
        normed = centred * inv
        R.mixed[r : r + 64, :] = normed
        R.xin[r : r + 64, :] = (normed * R.gain[...]).astype(BF)
    inv_std = jnp.concatenate(inv_parts, axis=0)
    to_experts(R.xin, R.xs)
    x_swap.send_all()
    g_on()
    R.xr[rows(tok, 16), :] = R.xs[rows(tok, 16), :]
    logits = nn(R.xin[...], R.router[...])
    gap = jnp.sum(logits * (pick1 - pick2), axis=1, keepdims=True)
    gate1 = 1.0 / (1.0 + jnp.exp(-gap))
    gate2 = 1.0 / (1.0 + jnp.exp(gap))
    low1 = gate1.astype(BF).astype(F32)
    low2 = gate2.astype(BF).astype(F32)
    R.ms[...] = nn((own1 * low1).T.astype(BF), at1.astype(BF)) + nn((own2 * low2).T.astype(BF), at2.astype(BF))
    m_swap.send_all()
    R.mr[rows(tok, 8), :] = R.ms[rows(tok, 8), :]
    for swap in (q_far, a_swap, g_swap):
        swap.sent_all()

    x_swap.arrive_all()
    unpack(R.xr, R.xall)
    xa_near.send_all()
    xa_far.send_all()
    m_swap.arrive_all()
    R.mall[src] = fold8(R.mr[...], jnp.sum)
    ma_swap.send_all()
    ga_swap.arrive_all()
    for c in range(0, 512, 128):
        R.backT[c : c + 128, :] = nt(R.f_out[c : c + 128, :], R.gall[...])
    R.kT[...] = jnp.where(seen_row, R.kh[...].astype(F32).T, 0.0).astype(BF)
    for swap in (x_swap, m_swap, ga_swap):
        swap.sent_all()
    ma_swap.arrive_all()

    for half, steps, xa_swap in ((x_lo, (1, 4), xa_near), (1 - x_lo, (4, 8), xa_far)):
        xa_swap.arrive_all()
        here = rows(half, 256)
        x_half = R.xall[here, :]
        m4 = half * 4
        gate_row = jnp.concatenate(
            [R.mall[m4][0:1, :] + R.mall[m4 + 1][0:1, :], R.mall[m4 + 2][0:1, :] + R.mall[m4 + 3][0:1, :]], axis=1
        )
        gate_acc = jnp.zeros((8, 256), F32)
        for c in range(0, 512, 128):
            value, slope = gelu_pair(nt(R.f_in[c : c + 128, :], x_half))
            act = value.astype(BF).astype(F32)
            back = R.backT[c : c + 128, here]
            gate_acc = gate_acc + fold8(back * act, jnp.sum)
            R.actg[c : c + 128, here] = (act * gate_row).astype(BF)
            dp = gate_row * back * slope
            R.dpT[c : c + 128, here] = dp.astype(BF)
            R.dpr[here, c : c + 128] = dp.T.astype(BF)
        gate_tot = jnp.sum(gate_acc, axis=0, keepdims=True)
        R.gps[half * 2] = jnp.broadcast_to(gate_tot[:, :HEAD], (8, HEAD))
        R.gps[half * 2 + 1] = jnp.broadcast_to(gate_tot[:, HEAD:], (8, HEAD))
        R.part[here, :] = nn(R.dpr[here, :], R.f_in[...]).astype(BF)
        each(steps[1], p_swap.send, steps[0])
        each(steps[1], gp_swap.send, steps[0])
    R.pr[src] = R.part[rows(src, 64), :]
    R.gpr[src] = R.gps[src // 2]
    stores = [
        pltpu.make_async_copy(a, b, R.io_sem.at[8 + i])
        for i, (a, b) in enumerate(
            (
                (R.d_fin, R.d_fin_hbm), (R.d_fout, R.d_fout_hbm), (R.dhid, R.dhid_hbm),
                (R.dw, R.dw_hbm), (R.d_router, R.d_router_hbm), (R.d_gain, R.d_gain_hbm),
            )
        )
    ]
    for c in range(0, 512, 128):
        R.d_fin[c : c + 128, :] = nn(R.dpT[c : c + 128, :], R.xall[...]).astype(BF)
        R.d_fout[c : c + 128, :] = nn(R.actg[c : c + 128, :], R.gall[...]).astype(BF)
    stores[0].start()
    stores[1].start()
    for swap in (xa_near, xa_far, ma_swap):
        swap.sent_all()
    gp_swap.arrive_all()
    R.gsum[...] = jnp.sum(R.gpr[...], axis=0)
    gb_swap.send_all()
    R.gb[rows(tok, 8), :] = R.gsum[...]
    p_swap.arrive_all()
    acc = None
    for b in range(4):
        blk = jnp.sum(R.pr[:, :, b * 256 : (b + 1) * 256].astype(F32), axis=0).astype(BF)
        term = nn(take[b].astype(F32).T.astype(BF), blk)
        acc = term if acc is None else acc + term
    R.ps[...] = acc.astype(BF)
    b_swap.send_all()
    R.br[rows(tok, 16), :] = R.ps[rows(tok, 16), :]

    gb_swap.arrive_all()
    first = jnp.where(lane % 8 == 0, 1.0, 0.0)
    got1 = nn(own1 * first, R.gb[...], precision=lax.Precision.HIGHEST)
    got2 = nn(own2 * first, R.gb[...], precision=lax.Precision.HIGHEST)
    grad1 = jnp.sum(got1 * at1, axis=1, keepdims=True)
    grad2 = jnp.sum(got2 * at2, axis=1, keepdims=True)
    logit_grad = gate1 * gate2 * (grad1 - grad2)
    column = (pick1 - pick2) * logit_grad
    col_hi = column.astype(BF)
    col_lo = (column - col_hi.astype(F32)).astype(BF)
    colT = column.T
    colT_hi = colT.astype(BF)
    colT_lo = (colT - colT_hi.astype(F32)).astype(BF)
    router_part = (nn(colT_hi, R.xin[...]) + nn(colT_lo, R.xin[...])).T.astype(BF)
    for t in range(N_TOK):
        R.r1[t] = router_part[t * 64 : (t + 1) * 64, :]
    r1_swap.send_all()
    R.r1r[tok] = R.r1[tok]
    for swap in (p_swap, gp_swap, gb_swap):
        swap.sent_all()
    b_swap.arrive_all()

    scaled_sum = jnp.zeros((ROWS, 1), F32)
    cross_sum = jnp.zeros((ROWS, 1), F32)
    scaled_all = []
    gain_rows = []
    for b in range(4):
        cut = slice(b * 256, (b + 1) * 256)
        mine = jnp.where(row_blk == b, R.hitT[...], zero)
        total = lax.dot_general(mine, R.br[...], (((0,), (0,)), ((), ())), preferred_element_type=F32)
        total = total + nt(col_hi, R.router[cut, :]) + nt(col_lo, R.router[cut, :])
        normed = R.mixed[:, cut]
        row = jnp.sum(total * normed, axis=0, keepdims=True)
        gain_rows += [row[:, :HEAD], row[:, HEAD:]]
        scaled = total * R.gain[:, cut]
        scaled_all.append(scaled)
        scaled_sum = scaled_sum + jnp.sum(scaled, axis=1, keepdims=True)
        cross_sum = cross_sum + jnp.sum(scaled * normed, axis=1, keepdims=True)
    mean1 = scaled_sum * (1.0 / WIDTH)
    mean2 = cross_sum * (1.0 / WIDTH)
    for b in range(4):
        cut = slice(b * 256, (b + 1) * 256)
        R.dhid[:, cut] = (
            R.dout[:, cut].astype(F32) + inv_std * (scaled_all[b] - mean1 - R.mixed[:, cut] * mean2)
        ).astype(BF)
    for h in range(N_SRC):
        R.og[h] = nt(R.dhid[...], R.w_out[h * HEAD : (h + 1) * HEAD, :]).astype(BF)
    og_near.send_all()
    og_far.send_all()
    R.g1[src] = jnp.concatenate(gain_rows, axis=0)
    g1_swap.send_all()
    stores[2].start()
    R.ogr[src] = R.og[src]

    for i in range(8):
        cut = slice(i * HEAD, (i + 1) * HEAD)
        w = nn(R.att[:, cut].astype(F32).T.astype(BF), R.dhid[...]).astype(BF)
        R.w1[i, 0] = w[:64]
        R.w1[i, 1] = w[64:]
    core_copy = remote(R.w1.at[:, 1 - c_me], R.c1, R.c_sem.at[0], R.c_sem.at[1], "tok", tok_step(tok, 1))
    core_copy.start()
    R.dka[...] = jnp.zeros_like(R.dka)
    R.dva[...] = jnp.zeros_like(R.dva)

    def backward_block(b):
        q, d_o = R.qh[b], R.ogr[b]
        d_wide = d_o.astype(F32)
        row_term = jnp.sum(d_wide.T * R.oT[b].astype(F32), axis=0, keepdims=True)
        top, inv = R.stat[b][0:1, :], R.stat[b][8:9, :]
        factor = inv * FACTOR
        scaled_d = (d_wide * R.stat[b][8:, :].T[:, 0:1]).astype(BF)
        for c in range(0, SRC_ALL, 128):
            s = nt(R.kh[c : c + 128, :], q)
            p = jnp.exp2((s - top) * EXP2_SCALE)
            R.pbuf[c : c + 128, :] = p.astype(BF)
            dp = nt(R.vh[c : c + 128, :], d_o)
            R.dsbuf[c : c + 128, :] = (p * ((dp - row_term) * factor)).astype(BF)
        R.dqs[b] = nn(R.kT[...], R.dsbuf[...]).T.astype(BF)
        R.dka[...] += nn(R.dsbuf[...], q)
        R.dva[...] += nn(R.pbuf[...], scaled_d)

    def backward_turn(k):
        backward_block(src_step(src, k, True))
        dq_swap.send(src_step(0, k, True))

    def turns(low, high):
        def step(k, carry):
            backward_turn(k)
            return carry

        lax.fori_loop(low, high, step, 0)

    backward_block(src)
    R.dqr[src] = R.dqs[src]
    core_copy.wait_recv()
    for i in range(8):
        piece = R.w1[i, c_me].astype(F32) + R.c1[i].astype(F32)
        R.ya[i] = piece[:, :512].astype(BF)
        R.wtmp[i] = piece[:, 512:]
    y_go(*ya_way)
    for s in range(N_SRC):
        R.sb[s] = jnp.concatenate([R.wtmp[i, s * 8 : (s + 1) * 8, :] for i in range(8)], axis=0).astype(BF)
    sb_swap.send_all()
    R.yar[y_me] = R.ya[pl.ds(y_me * 2, 2)]
    R.sbr[src] = R.sb[src]
    r1_swap.arrive_all()
    R.r2[src] = jnp.sum(R.r1r[...].astype(F32), axis=0).astype(BF)
    r2_swap.send_all()
    og_near.arrive_all()
    turns(1, 4)
    g1_swap.arrive_all()
    R.g2[tok] = jnp.sum(R.g1[...], axis=0)
    g2_swap.send_all()
    og_far.arrive_all()
    turns(4, 6)
    y_arrive(*ya_way)
    a0 = jnp.sum(R.yar[:, 0].astype(F32), axis=0)
    a1 = jnp.sum(R.yar[:, 1].astype(F32), axis=0)
    for s in range(N_SRC):
        R.sa[s] = jnp.concatenate([a0[s * 8 : (s + 1) * 8, :], a1[s * 8 : (s + 1) * 8, :]], axis=0).astype(BF)
    sa_swap.send_all()
    R.sar[src] = R.sa[src]
    sb_swap.arrive_all()
    sums = jnp.sum(R.sbr[...].astype(F32), axis=0)
    for y in range(4):
        R.yb[y] = sums[y * 16 : (y + 1) * 16, :].astype(BF)
    y_go(*yb_way)
    R.ybr[y_me] = R.yb[y_me]
    r2_swap.arrive_all()
    R.r3[tok] = jnp.sum(R.r2[...].astype(F32), axis=0).astype(BF)
    r3_swap.send_all()
    turns(6, 8)
    R.dks[...] = jnp.where(seen, R.dka[...], 0.0).astype(BF)
    dk_swap.send_all()
    R.dvs[...] = jnp.where(seen, R.dva[...], 0.0).astype(BF)
    dv_swap.send_all()
    R.dkr[src] = R.dks[rows(src, 128), :]
    R.dvr[src] = R.dvs[rows(src, 128), :]
    sa_swap.arrive_all()
    y_arrive(*yb_way)
    sums_a = jnp.sum(R.sar[...].astype(F32), axis=0)
    sums_b = jnp.sum(R.ybr[...].astype(F32), axis=0)
    for x in range(2):
        R.x5[x, :, :512] = sums_a[x * 8 : (x + 1) * 8, :]
        R.x5[x, :, 512:] = sums_b[x * 8 : (x + 1) * 8, :]
    x_copy = remote(R.x5.at[1 - x_me], R.x5.at[2], R.xh_sem.at[0], R.xh_sem.at[1], "tok", tok_step(tok, 2))
    x_copy.start()
    for swap in (b_swap, r1_swap, og_near, og_far, r2_swap, g1_swap, sb_swap, sa_swap):
        swap.sent_all()
    core_copy.wait_send()
    y_sent(*ya_way)
    y_sent(*yb_way)

    def keep(swap, held, out, sem):
        swap.arrive_all()
        for h in range(N_SRC):
            pltpu.make_async_copy(held.at[h], out.at[:, pl.ds(h * HEAD, HEAD)], sem).start()

    keep(dq_swap, R.dqr, R.dq_hbm, R.io_sem.at[14])
    g2_swap.arrive_all()
    R.d_gain[...] = jnp.sum(R.g2[...], axis=0)
    r3_swap.arrive_all()
    for t in range(N_TOK):
        R.d_router[t * 64 : (t + 1) * 64, :] = R.r3[t].astype(F32)
    stores[4].start()
    stores[5].start()
    x_copy.wait_recv()
    R.dw[...] = R.x5[x_me] + R.x5[2]
    stores[3].start()
    keep(dk_swap, R.dkr, R.dk_hbm, R.io_sem.at[15])
    keep(dv_swap, R.dvr, R.dv_hbm, R.io_sem.at[16])
    for swap in (r3_swap, g2_swap, dq_swap, dk_swap, dv_swap):
        swap.sent_all()
    x_copy.wait_send()
    bulk_wait(R.dqr, R.io_sem.at[14])
    bulk_wait(R.dkr, R.io_sem.at[15])
    bulk_wait(R.dvr, R.io_sem.at[16])
    for copy in stores:
        copy.wait()


def hand_over_kernel(*refs):
    count = (len(refs) - 1) // 3
    given, out, held, sem = refs[:count], refs[count : 2 * count], refs[2 * count : 3 * count], refs[-1]
    loads = [pltpu.make_async_copy(given[i], held[i], sem.at[0, i]) for i in range(count)]
    stores = [pltpu.make_async_copy(held[i], out[i], sem.at[1, i]) for i in range(count)]
    for copy in loads:
        copy.start()
    for load, store in zip(loads, stores):
        load.wait()
        store.start()
    for copy in stores:
        copy.wait()


VMEM = pl.BlockSpec(memory_space=pltpu.VMEM)
SMEM = pl.BlockSpec(memory_space=pltpu.SMEM)
HBM = pl.BlockSpec(memory_space=pl.ANY)


def on_device(
    hidden_in, d_out, queries, keys, values, source_len, out_weight, norm_gain, router,
    expert_ids, expert_slots, fc_in, fc_out,
):
    shapes = tuple(
        jax.ShapeDtypeStruct(s, d)
        for s, d in (
            ((ROWS, WIDTH), BF), ((ROWS, WIDTH), BF), ((HEAD, WIDTH), BF), ((HEAD, WIDTH), BF), ((8, WIDTH), F32),
            ((WIDTH, HEAD), F32), ((8, HEAD), F32), ((512, WIDTH), BF), ((512, WIDTH), BF),
        )
    )
    outs = pl.pallas_call(
        block_kernel,
        out_shape=shapes,
        in_specs=[SMEM] + [VMEM] * 4 + [HBM] * 8,
        out_specs=(HBM,) * 9,
        scratch_shapes=list(SCRATCH.values()),
        compiler_params=pltpu.CompilerParams(
            collective_id=1, has_side_effects=True, vmem_limit_bytes=58 * 1024 * 1024
        ),
    )(
        source_len, norm_gain[None], router, expert_ids.T, expert_slots.T, queries, keys[0], values[0], d_out,
        hidden_in, out_weight, fc_in[0], fc_out[0],
    )
    dhid, dq, dk, dv, dw, d_router, d_gain, d_fin, d_fout = pl.pallas_call(
        hand_over_kernel,
        out_shape=shapes,
        in_specs=[HBM] * 9,
        out_specs=(HBM,) * 9,
        scratch_shapes=[pltpu.VMEM(s.shape, s.dtype) for s in shapes] + [sems(2, 9)],
        compiler_params=pltpu.CompilerParams(vmem_limit_bytes=58 * 1024 * 1024),
    )(*outs)
    return dhid, dq, dk[None], dv[None], dw, d_router, d_gain.reshape(-1), d_fin[None], d_fout[None]


def solution(mesh):
    return jax.shard_map(
        on_device,
        mesh=mesh,
        in_specs=(
            P(("tok", "src"), None), P(("tok", "src"), None), P(("tok", "src"), None),
            P("tok", "src", None), P("tok", "src", None), P(), P(), P(), P(),
            P(("tok", "src"), None), P(("tok", "src"), None), P("tok", "src", None), P("tok", "src", None),
        ),
        out_specs=(
            P(("tok", "src"), None), P(("tok", "src"), None), P("tok", "src", None), P("tok", "src", None),
            P(("tok", "src"), None), P(), P(), P("tok", "src", None), P("tok", "src", None),
        ),
        check_vma=False,
    )
```

time: 1240 us -> 126 us (0.10)
  waiting for transfers between devices: 995 us -> 0 us
  Pallas kernels: 0 us -> 124 us
  blocking collectives: 104 us -> 0 us
  matrix products: 57.7 us -> 0 us
  local copies, waits for them, and re-layouts: 34.6 us -> 0 us
  starting transfers between devices: 17.1 us -> 0 us
  other arithmetic: 14.4 us -> 0 us
  between operations: 15.2 us -> 0.82 us
    reduce_scatter x4 -> x0, waiting for transfers between devices: 775 us -> none  [the longest x1 647 us: on_device(): lax.psum_scatter(jnp.einsum('th,td->hd', attended, d_hidden, preferred_el...]
    all_gather x4 -> x0, waiting for transfers between devices: 134 us -> none  [the longest x1 43.9 us: on_device(): lax.all_gather(keys[0], 'src', axis=0, tiled=True)]
    pallas_call x0 -> x2, Pallas kernels: none -> 124 us  [the longest x1 120 us: on_device(): pl.pallas_call(block_kernel, out_shape=shapes, in_specs=[SMEM] + [VMEM] *...]
    psum x1 -> x0, blocking collectives: 62.7 us -> none  [on_device(): d_router, d_gain = lax.psum((router_part, gain_part), ('tok', 'src'))]
    dot_general x21 -> x0, matrix products: 49.6 us -> none  [the longest x1 6.24 us: on_device(): jnp.einsum('thd,shd->hts', out_heads, value_all, preferred_element_type=j...]
    unnamed x11 -> x0, waiting for transfers between devices: 36.9 us -> none
    psum x1 -> x0, waiting for transfers between devices: 30.5 us -> none  [on_device(): d_router, d_gain = lax.psum((router_part, gain_part), ('tok', 'src'))]
    all_to_all x2 -> x0, blocking collectives: 25.3 us -> none  [the longest x1 14.5 us: on_device(): lax.all_to_all(sent_in, 'tok', split_axis=0, concat_axis=1, tiled=True)]
  transfers between devices with their start and end apart: 13 -> 0, of which waited for: 13 -> 0; matrix products, arithmetic and copies ran while one was open for 6% -> 0% of each run, Pallas kernels for 0% -> 0%
where the time goes in v2:
time: 126 us; the launch traced here: 125 us
  Pallas kernels  124 us (98%)
    pallas_call x1, Pallas kernels, on_device(): pl.pallas_call(block_kernel, out_shape=shapes, in_specs=[SMEM] + [VMEM] *...  120 us
    pallas_call x1, Pallas kernels, on_device(): pl.pallas_call(hand_over_kernel, out_shape=shapes, in_specs=[HBM] * 9, ou...  3.88 us

profile of v2, /device:TPU:0, one launch (start us, length us, event | category | flops | bytes accessed | tf_op | source)
XLA Modules:
  0.0 125.0 jit_solution(10781973276451484545)
XLA Ops:
  0.6 120.3 %shard_map.196 = (bf16[256,1024]{1,0:T(8,128)(2,1)}, bf16[256,1024]{1,0:T(8,128)(2,1)}, bf16[128,1024]{1,0:T(8,128)(2,1)}, bf16[128,1024]{1,0:T(8,128)(2,1)}, f3...) custom-call(s32[16]{0:T(128)} %refs_0_.1, ...), custom_call_target="tpu_custom_call" | custom-call | tf_op jit(solution)/shard_map/pallas_call | solution.py:672
  120.9 3.9 %shard_map.197 = (bf16[256,1024]{1,0:T(8,128)(2,1)}, bf16[256,1024]{1,0:T(8,128)(2,1)}, bf16[128,1024]{1,0:T(8,128)(2,1)}, bf16[128,1024]{1,0:T(8,128)(2,1)}, f3...) custom-call(bf16[256,1024]{1,0:T(8,128)(2,1)} %get-tuple-element.27., ...), custom_call_target="tpu_custom_call" | custom-call | tf_op jit(solution)/shard_map/pallas_call | solution.py:685

commit v3 on v2

--- a/solution.py
+++ b/solution.py
@@ -73,7 +73,8 @@
 
 
 class Swap:
-    def __init__(self, axis, me, sems, source, target, blocks, low=1, high=None):
+    def __init__(self, axis, me, sems, source, target, blocks, low=1, high=None, pick=None):
+        self.pick = pick or (lambda i: i)
         self.axis, self.me, self.sems = axis, me, sems
         self.source, self.target = source, target
         self.low, self.high = low, high or (N_SRC if axis == "src" else N_TOK)
@@ -81,7 +82,7 @@
         self.step = src_step if axis == "src" else tok_step
 
     def send(self, k):
-        to = self.step(self.me, k)
+        to = self.step(self.me, self.pick(k))
         remote(self.source(to), self.target(self.me), self.sems.at[0], self.sems.at[1], self.axis, to).start()
 
     def send_all(self):
@@ -92,6 +93,14 @@
 
     def sent_all(self):
         bulk_wait(self.held, self.sems.at[0])
+
+
+def near_step(i):
+    return 2 * i - 1 - (i - 1) // 2
+
+
+def far_step(i):
+    return i - 2 + 2 * ((i - 2) // 3)
 
 
 def bulk_wait(ref, sem):
@@ -133,15 +142,15 @@
     hid=vm(ROWS, WIDTH), w_out=vm(WIDTH, WIDTH), f_in=vm(512, WIDTH), f_out=vm(512, WIDTH),
     qh=vm(8, ROWS, HEAD), kh=vm(SRC_ALL, HEAD), vh=vm(SRC_ALL, HEAD), att_in=vm(8, ROWS, HEAD),
     att_send=vm(8, ROWS, HEAD), vT=vm(HEAD + 16, SRC_ALL), kT=vm(HEAD, SRC_ALL), sbuf=vm(SRC_ALL, ROWS, dtype=F32),
-    pbuf=vm(SRC_ALL, ROWS), dsbuf=vm(SRC_ALL, ROWS),
-    oT=vm(8, HEAD, ROWS), stat=vm(8, 16, ROWS, dtype=F32), att=vm(ROWS, WIDTH),
+    pall=vm(8, SRC_ALL, ROWS), dsbuf=vm(SRC_ALL, ROWS),
+    oT=vm(8, HEAD, ROWS), stat=vm(8, 8, ROWS, dtype=F32), att=vm(ROWS, WIDTH),
     mixed=vm(ROWS, WIDTH, dtype=F32), xin=vm(ROWS, WIDTH), hitT=vm(ROWS, ROWS),
     xs=vm(ROWS, ROWS), gs=vm(ROWS, ROWS), ms=vm(HEAD, HEAD, dtype=F32),
     xr=vm(ROWS, ROWS), gr=vm(ROWS, ROWS), mr=vm(HEAD, HEAD, dtype=F32),
-    xall=vm(512, WIDTH), gall=vm(512, WIDTH), mall=vm(8, 8, HEAD, dtype=F32),
+    xall=vm(2, 256, WIDTH), gall=vm(2, 256, WIDTH), mall=vm(8, 16, HEAD, dtype=F32),
     backT=vm(512, 512, dtype=F32), actg=vm(512, 512), dpT=vm(512, 512), dpr=vm(512, 512),
-    part=vm(512, WIDTH), pr=vm(8, 64, WIDTH), gps=vm(4, 8, HEAD, dtype=F32), gpr=vm(8, 8, HEAD, dtype=F32),
-    ps=vm(ROWS, ROWS), br=vm(ROWS, ROWS), gsum=vm(8, HEAD, dtype=F32), gb=vm(HEAD, HEAD, dtype=F32),
+    part=vm(2, 256, WIDTH), pr=vm(8, 64, WIDTH), gps=vm(2, 2, 8, HEAD, dtype=F32), gpr=vm(8, 2, 8, HEAD, dtype=F32),
+    ps=vm(ROWS, ROWS), br=vm(ROWS, ROWS), gsum=vm(2, 8, HEAD, dtype=F32), gb=vm(HEAD, HEAD, dtype=F32),
     dhid=vm(ROWS, WIDTH), d_fin=vm(512, WIDTH), d_fout=vm(512, WIDTH),
     og=vm(8, ROWS, HEAD), ogr=vm(8, ROWS, HEAD), dqs=vm(8, ROWS, HEAD), dqr=vm(8, ROWS, HEAD),
     dka=vm(SRC_ALL, HEAD, dtype=F32), dva=vm(SRC_ALL, HEAD, dtype=F32), dks=vm(SRC_ALL, HEAD), dvs=vm(SRC_ALL, HEAD),
@@ -155,7 +164,7 @@
     dout=vm(ROWS, WIDTH),
     k_sem=sems(2), v_sem=sems(2), qn_sem=sems(2), qf_sem=sems(2), a_sem=sems(2), x_sem=sems(2), g_sem=sems(2),
     m_sem=sems(2), xan_sem=sems(2), xaf_sem=sems(2), ga_sem=sems(2), ma_sem=sems(2), p_sem=sems(2),
-    gp_sem=sems(2), b_sem=sems(2), gb_sem=sems(2), ogn_sem=sems(2), ogf_sem=sems(2), dq_sem=sems(2),
+    gp_sem=sems(2), p2_sem=sems(2), b_sem=sems(2), gb_sem=sems(2), ogn_sem=sems(2), ogf_sem=sems(2), dq_sem=sems(2),
     dk_sem=sems(2), dv_sem=sems(2), c_sem=sems(2), xh_sem=sems(2), ya_sem=sems(2), yb_sem=sems(2), sa_sem=sems(2),
     sb_sem=sems(2), r1_sem=sems(2), r2_sem=sems(2), r3_sem=sems(2), g1_sem=sems(2), g2_sem=sems(2),
     io_sem=sems(17),
@@ -214,21 +223,35 @@
     k_swap = by_src(R.k_sem, lambda p: R.k.at[:, lanes(p)], at_rows(R.kh, 128), first(R.kh, 128))
     v_swap = by_src(R.v_sem, lambda p: R.v.at[:, lanes(p)], at_rows(R.vh, 128), first(R.vh, 128))
     q_way = lambda p: R.q.at[:, lanes(p)], at(R.qh), first(R.qh)
-    q_near, q_far = by_src(R.qn_sem, *q_way, 1, 4), by_src(R.qf_sem, *q_way, 4, 8)
+    q_near, q_far = by_src(R.qn_sem, *q_way, 1, 4, near_step), by_src(R.qf_sem, *q_way, 4, 8, far_step)
     a_swap = by_src(R.a_sem, at(R.att_send), at(R.att_in), first(R.att_in))
     x_swap = by_tok(R.x_sem, at_rows(R.xs, 16), at_rows(R.xr, 16), first(R.xr, 16))
     g_swap = by_tok(R.g_sem, at_rows(R.gs, 16), at_rows(R.gr, 16), first(R.gr, 16))
     m_swap = by_tok(R.m_sem, at_rows(R.ms, 8), at_rows(R.mr, 8), first(R.mr, 8))
-    xa_way = lambda p: R.xall.at[rows(src, 64)], at_rows(R.xall, 64), first(R.xall, 64)
-    xa_near, xa_far = by_src(R.xan_sem, *xa_way, 1, 4), by_src(R.xaf_sem, *xa_way, 4, 8)
-    ga_swap = by_src(R.ga_sem, lambda p: R.gall.at[rows(src, 64)], at_rows(R.gall, 64), first(R.gall, 64))
+    def xa_half(sem, half):
+        return by_src(
+            sem, lambda p: R.xall.at[half, rows(src, 32)], lambda i: R.xall.at[half, rows(i, 32)],
+            lambda n: R.xall.at[half, pl.ds(0, n * 32)],
+        )
+
+    def p_half(sem, half):
+        return by_src(
+            sem, lambda p: R.part.at[half, rows(p, 32)], lambda i: R.pr.at[i, pl.ds(half * 32, 32)],
+            lambda n: R.pr.at[pl.ds(0, n), pl.ds(half * 32, 32)],
+        )
+
+    xa_swaps = xa_half(R.xan_sem, 0), xa_half(R.xaf_sem, 1)
+    p_swaps = p_half(R.p_sem, 0), p_half(R.p2_sem, 1)
+    ga_swap = by_src(
+        R.ga_sem, lambda p: R.gall.at[:, rows(src, 32)], lambda i: R.gall.at[:, rows(i, 32)],
+        lambda n: R.gall.at[:, pl.ds(0, n * 32)],
+    )
     ma_swap = by_src(R.ma_sem, lambda p: R.mall.at[src], at(R.mall), first(R.mall))
-    p_swap = by_src(R.p_sem, at_rows(R.part, 64), at(R.pr), first(R.pr))
-    gp_swap = by_src(R.gp_sem, lambda p: R.gps.at[p // 2], at(R.gpr), first(R.gpr))
+    gp_swap = by_src(R.gp_sem, lambda p: R.gps.at[p // 4], at(R.gpr), first(R.gpr))
     b_swap = by_tok(R.b_sem, at_rows(R.ps, 16), at_rows(R.br, 16), first(R.br, 16))
-    gb_swap = by_tok(R.gb_sem, lambda p: R.gsum, at_rows(R.gb, 8), first(R.gb, 8))
+    gb_swap = by_tok(R.gb_sem, lambda p: R.gsum.at[p // 8], at_rows(R.gb, 8), first(R.gb, 8))
     og_way = at(R.og), at(R.ogr), first(R.ogr)
-    og_near, og_far = by_src(R.ogn_sem, *og_way, 1, 4), by_src(R.ogf_sem, *og_way, 4, 8)
+    og_near, og_far = by_src(R.ogn_sem, *og_way, 1, 4, near_step), by_src(R.ogf_sem, *og_way, 4, 8, far_step)
     dq_swap = by_src(R.dq_sem, at(R.dqs), at(R.dqr), first(R.dqr))
     dk_swap = by_src(R.dk_sem, at_rows(R.dks, 128), at(R.dkr), first(R.dkr))
     dv_swap = by_src(R.dv_sem, at_rows(R.dvs, 128), at(R.dvr), first(R.dvr))
@@ -308,14 +331,12 @@
         top = jnp.max(top, axis=0, keepdims=True)
         for c in range(0, SRC_ALL, 128):
             p = jnp.exp2((R.sbuf[c : c + 128, :] - top) * EXP2_SCALE)
-            R.pbuf[c : c + 128, :] = p.astype(BF)
-        summed = nn(R.vT[...], R.pbuf[...])
+            R.pall[b, c : c + 128, :] = p.astype(BF)
+        summed = nn(R.vT[...], R.pall[b])
         inv = 1.0 / summed[HEAD : HEAD + 1, :]
         oT = summed[:HEAD, :] * inv
         R.oT[b] = oT.astype(BF)
-        R.stat[b] = jnp.concatenate(
-            [jnp.broadcast_to(top, (8, ROWS)), jnp.broadcast_to(inv, (8, ROWS))], axis=0
-        )
+        R.stat[b] = jnp.broadcast_to(inv, (8, ROWS))
         R.att_send[b] = oT.T.astype(BF)
 
     i64, j256 = iota((64, ROWS), 0), iota((64, ROWS), 1)
@@ -323,7 +344,9 @@
 
     def unpack(got, out):
         for b in range(4):
-            out[rows(src, 64), b * 256 : (b + 1) * 256] = nn(take[b], got[...]).astype(BF)
+            block = nn(take[b], got[...]).astype(BF)
+            out[0, rows(src, 32), b * 256 : (b + 1) * 256] = block[:32]
+            out[1, rows(src, 32), b * 256 : (b + 1) * 256] = block[32:]
 
     def g_on():
         g_swap.arrive_all()
@@ -338,9 +361,9 @@
         a_swap.send(src_step(0, k, True))
 
     q_near.arrive_all()
-    each(4, forward_turn)
+    each(4, lambda i: forward_turn(near_step(i)))
     q_far.arrive_all()
-    each(8, forward_turn, 4)
+    each(8, lambda i: forward_turn(far_step(i)), 4)
 
     id_cols = jnp.concatenate([R.ids[...], R.slots[...], R.ids[...], R.slots[...]], axis=0).astype(F32).T
     id_cols = id_cols.astype(jnp.int32)
@@ -349,7 +372,7 @@
     pick1 = jnp.where(id1 == lane, 1.0, 0.0)
     pick2 = jnp.where(id2 == lane, 1.0, 0.0)
     live1, live2 = slot1 >= 0, slot2 >= 0
-    base = (src % 2) * 64 + tok * CAP
+    base = (src % 4) * 32 + (tok % 8) * CAP
     own1 = jnp.where(live1 & (id1 < N_TOK) & (id1 == lane // 8), 1.0, 0.0)
     own2 = jnp.where(live2 & (id2 < N_TOK) & (id2 == lane // 8), 1.0, 0.0)
     at1 = jnp.where(live1 & (lane == base + slot1), 1.0, 0.0)
@@ -389,27 +412,26 @@
 
     x_swap.arrive_all()
     unpack(R.xr, R.xall)
-    xa_near.send_all()
-    xa_far.send_all()
+    xa_swaps[0].send_all()
     m_swap.arrive_all()
-    R.mall[src] = fold8(R.mr[...], jnp.sum)
+    R.mall[src] = jnp.concatenate([fold8(R.mr[:64, :], jnp.sum), fold8(R.mr[64:, :], jnp.sum)], axis=0)
     ma_swap.send_all()
     ga_swap.arrive_all()
     for c in range(0, 512, 128):
-        R.backT[c : c + 128, :] = nt(R.f_out[c : c + 128, :], R.gall[...])
+        R.backT[c : c + 128, :] = nt(R.f_out[c : c + 128, :], R.gall[...].reshape(512, WIDTH))
     R.kT[...] = jnp.where(seen_row, R.kh[...].astype(F32).T, 0.0).astype(BF)
+    xa_swaps[0].sent_all()
+    xa_swaps[1].send_all()
     for swap in (x_swap, m_swap, ga_swap):
         swap.sent_all()
     ma_swap.arrive_all()
 
-    for half, steps, xa_swap in ((x_lo, (1, 4), xa_near), (1 - x_lo, (4, 8), xa_far)):
-        xa_swap.arrive_all()
-        here = rows(half, 256)
-        x_half = R.xall[here, :]
-        m4 = half * 4
-        gate_row = jnp.concatenate(
-            [R.mall[m4][0:1, :] + R.mall[m4 + 1][0:1, :], R.mall[m4 + 2][0:1, :] + R.mall[m4 + 3][0:1, :]], axis=1
-        )
+    for half in range(2):
+        xa_swaps[half].arrive_all()
+        here = slice(half * 256, (half + 1) * 256)
+        x_half = R.xall[half]
+        gates = jnp.sum(R.mall[:, half * 8 : half * 8 + 8, :].reshape(2, 4, 8, HEAD), axis=1)
+        gate_row = jnp.concatenate([gates[0, 0:1, :], gates[1, 0:1, :]], axis=1)
         gate_acc = jnp.zeros((8, 256), F32)
         for c in range(0, 512, 128):
             value, slope = gelu_pair(nt(R.f_in[c : c + 128, :], x_half))
@@ -421,13 +443,13 @@
             R.dpT[c : c + 128, here] = dp.astype(BF)
             R.dpr[here, c : c + 128] = dp.T.astype(BF)
         gate_tot = jnp.sum(gate_acc, axis=0, keepdims=True)
-        R.gps[half * 2] = jnp.broadcast_to(gate_tot[:, :HEAD], (8, HEAD))
-        R.gps[half * 2 + 1] = jnp.broadcast_to(gate_tot[:, HEAD:], (8, HEAD))
-        R.part[here, :] = nn(R.dpr[here, :], R.f_in[...]).astype(BF)
-        each(steps[1], p_swap.send, steps[0])
-        each(steps[1], gp_swap.send, steps[0])
-    R.pr[src] = R.part[rows(src, 64), :]
-    R.gpr[src] = R.gps[src // 2]
+        R.gps[0, half] = jnp.broadcast_to(gate_tot[:, :HEAD], (8, HEAD))
+        R.gps[1, half] = jnp.broadcast_to(gate_tot[:, HEAD:], (8, HEAD))
+        R.part[half] = nn(R.dpr[here, :], R.f_in[...]).astype(BF)
+        p_swaps[half].send_all()
+        R.pr[src, half * 32 : half * 32 + 32, :] = R.part[half, rows(src, 32), :]
+    gp_swap.send_all()
+    R.gpr[src] = R.gps[src // 4]
     stores = [
         pltpu.make_async_copy(a, b, R.io_sem.at[8 + i])
         for i, (a, b) in enumerate(
@@ -438,17 +460,18 @@
         )
     ]
     for c in range(0, 512, 128):
-        R.d_fin[c : c + 128, :] = nn(R.dpT[c : c + 128, :], R.xall[...]).astype(BF)
-        R.d_fout[c : c + 128, :] = nn(R.actg[c : c + 128, :], R.gall[...]).astype(BF)
+        R.d_fin[c : c + 128, :] = nn(R.dpT[c : c + 128, :], R.xall[...].reshape(512, WIDTH)).astype(BF)
+        R.d_fout[c : c + 128, :] = nn(R.actg[c : c + 128, :], R.gall[...].reshape(512, WIDTH)).astype(BF)
     stores[0].start()
     stores[1].start()
-    for swap in (xa_near, xa_far, ma_swap):
+    for swap in (xa_swaps[1], ma_swap):
         swap.sent_all()
     gp_swap.arrive_all()
     R.gsum[...] = jnp.sum(R.gpr[...], axis=0)
     gb_swap.send_all()
-    R.gb[rows(tok, 8), :] = R.gsum[...]
-    p_swap.arrive_all()
+    R.gb[rows(tok, 8), :] = R.gsum[tok // 8]
+    p_swaps[0].arrive_all()
+    p_swaps[1].arrive_all()
     acc = None
     for b in range(4):
         blk = jnp.sum(R.pr[:, :, b * 256 : (b + 1) * 256].astype(F32), axis=0).astype(BF)
@@ -476,7 +499,7 @@
         R.r1[t] = router_part[t * 64 : (t + 1) * 64, :]
     r1_swap.send_all()
     R.r1r[tok] = R.r1[tok]
-    for swap in (p_swap, gp_swap, gb_swap):
+    for swap in (*p_swaps, gp_swap, gb_swap):
         swap.sent_all()
     b_swap.arrive_all()
 
@@ -526,29 +549,23 @@
         q, d_o = R.qh[b], R.ogr[b]
         d_wide = d_o.astype(F32)
         row_term = jnp.sum(d_wide.T * R.oT[b].astype(F32), axis=0, keepdims=True)
-        top, inv = R.stat[b][0:1, :], R.stat[b][8:9, :]
-        factor = inv * FACTOR
-        scaled_d = (d_wide * R.stat[b][8:, :].T[:, 0:1]).astype(BF)
+        factor = R.stat[b][0:1, :] * FACTOR
+        scaled_d = (d_wide * R.stat[b].T[:, 0:1]).astype(BF)
         for c in range(0, SRC_ALL, 128):
-            s = nt(R.kh[c : c + 128, :], q)
-            p = jnp.exp2((s - top) * EXP2_SCALE)
-            R.pbuf[c : c + 128, :] = p.astype(BF)
+            p = R.pall[b, c : c + 128, :].astype(F32)
             dp = nt(R.vh[c : c + 128, :], d_o)
             R.dsbuf[c : c + 128, :] = (p * ((dp - row_term) * factor)).astype(BF)
         R.dqs[b] = nn(R.kT[...], R.dsbuf[...]).T.astype(BF)
         R.dka[...] += nn(R.dsbuf[...], q)
-        R.dva[...] += nn(R.pbuf[...], scaled_d)
+        R.dva[...] += nn(R.pall[b], scaled_d)
 
     def backward_turn(k):
         backward_block(src_step(src, k, True))
         dq_swap.send(src_step(0, k, True))
 
     def turns(low, high):
-        def step(k, carry):
-            backward_turn(k)
-            return carry
-
-        lax.fori_loop(low, high, step, 0)
+        pick = near_step if high <= 4 else far_step
+        each(high, lambda i: backward_turn(pick(i)), low)
 
     backward_block(src)
     R.dqr[src] = R.dqs[src]
@@ -571,6 +588,9 @@
     g1_swap.arrive_all()
     R.g2[tok] = jnp.sum(R.g1[...], axis=0)
     g2_swap.send_all()
+    r2_swap.arrive_all()
+    R.r3[tok] = jnp.sum(R.r2[...].astype(F32), axis=0).astype(BF)
+    r3_swap.send_all()
     og_far.arrive_all()
     turns(4, 6)
     y_arrive(*ya_way)
@@ -586,9 +606,6 @@
         R.yb[y] = sums[y * 16 : (y + 1) * 16, :].astype(BF)
     y_go(*yb_way)
     R.ybr[y_me] = R.yb[y_me]
-    r2_swap.arrive_all()
-    R.r3[tok] = jnp.sum(R.r2[...].astype(F32), axis=0).astype(BF)
-    r3_swap.send_all()
     turns(6, 8)
     R.dks[...] = jnp.where(seen, R.dka[...], 0.0).astype(BF)
     dk_swap.send_all()
@@ -642,8 +659,9 @@
 def hand_over_kernel(*refs):
     count = (len(refs) - 1) // 3
     given, out, held, sem = refs[:count], refs[count : 2 * count], refs[2 * count : 3 * count], refs[-1]
-    loads = [pltpu.make_async_copy(given[i], held[i], sem.at[0, i]) for i in range(count)]
-    stores = [pltpu.make_async_copy(held[i], out[i], sem.at[1, i]) for i in range(count)]
+    order = sorted(range(count), key=lambda i: -given[i].size)
+    loads = [pltpu.make_async_copy(given[i], held[i], sem.at[0, i]) for i in order]
+    stores = [pltpu.make_async_copy(held[i], out[i], sem.at[1, i]) for i in order]
     for copy in loads:
         copy.start()
     for load, store in zip(loads, stores):

time: 126 us -> 124 us (0.984)
  no operation moved by 1% of the time
where the time goes in v3:
time: 124 us
  Pallas kernels  123 us (99%)
    pallas_call x1, Pallas kernels, on_device(): pl.pallas_call(block_kernel, out_shape=shapes, in_specs=[SMEM] + [VMEM] *...  119 us
    pallas_call x1, Pallas kernels, on_device(): pl.pallas_call(hand_over_kernel, out_shape=shapes, in_specs=[HBM] * 9, ou...  3.4 us

profile of v3, /device:TPU:0, one launch (start us, length us, event | category | flops | bytes accessed | tf_op | source)
XLA Modules:
  0.0 123.7 jit_solution(11501291224462752856)
XLA Ops:
  0.6 119.5 %shard_map.196 = (bf16[256,1024]{1,0:T(8,128)(2,1)}, bf16[256,1024]{1,0:T(8,128)(2,1)}, bf16[128,1024]{1,0:T(8,128)(2,1)}, bf16[128,1024]{1,0:T(8,128)(2,1)}, f3...) custom-call(s32[16]{0:T(128)} %refs_0_.1, ...), custom_call_target="tpu_custom_call" | custom-call | tf_op jit(solution)/shard_map/pallas_call | solution.py:690
  120.1 3.4 %shard_map.197 = (bf16[256,1024]{1,0:T(8,128)(2,1)}, bf16[256,1024]{1,0:T(8,128)(2,1)}, bf16[128,1024]{1,0:T(8,128)(2,1)}, bf16[128,1024]{1,0:T(8,128)(2,1)}, f3...) custom-call(bf16[256,1024]{1,0:T(8,128)(2,1)} %get-tuple-element.27., ...), custom_call_target="tpu_custom_call" | custom-call | tf_op jit(solution)/shard_map/pallas_call | solution.py:703

commit v4 on v3

--- a/solution.py
+++ b/solution.py
@@ -529,7 +529,6 @@
     for h in range(N_SRC):
         R.og[h] = nt(R.dhid[...], R.w_out[h * HEAD : (h + 1) * HEAD, :]).astype(BF)
     og_near.send_all()
-    og_far.send_all()
     R.g1[src] = jnp.concatenate(gain_rows, axis=0)
     g1_swap.send_all()
     stores[2].start()
@@ -542,6 +541,8 @@
         R.w1[i, 1] = w[64:]
     core_copy = remote(R.w1.at[:, 1 - c_me], R.c1, R.c_sem.at[0], R.c_sem.at[1], "tok", tok_step(tok, 1))
     core_copy.start()
+    og_near.sent_all()
+    og_far.send_all()
     R.dka[...] = jnp.zeros_like(R.dka)
     R.dva[...] = jnp.zeros_like(R.dva)
 
@@ -622,7 +623,7 @@
         R.x5[x, :, 512:] = sums_b[x * 8 : (x + 1) * 8, :]
     x_copy = remote(R.x5.at[1 - x_me], R.x5.at[2], R.xh_sem.at[0], R.xh_sem.at[1], "tok", tok_step(tok, 2))
     x_copy.start()
-    for swap in (b_swap, r1_swap, og_near, og_far, r2_swap, g1_swap, sb_swap, sa_swap):
+    for swap in (b_swap, r1_swap, og_far, r2_swap, g1_swap, sb_swap, sa_swap):
         swap.sent_all()
     core_copy.wait_send()
     y_sent(*ya_way)

time: 124 us -> 123 us (level)
  Pallas kernels: 123 us -> 121 us
    pallas_call x1, Pallas kernels: 119 us -> 118 us  [on_device(): pl.pallas_call(block_kernel, out_shape=shapes, in_specs=[SMEM] + [VMEM] *...]
where the time goes in v4:
time: 123 us; the launch traced here: 122 us
  Pallas kernels  121 us (98%)
    pallas_call x1, Pallas kernels, on_device(): pl.pallas_call(block_kernel, out_shape=shapes, in_specs=[SMEM] + [VMEM] *...  118 us
    pallas_call x1, Pallas kernels, on_device(): pl.pallas_call(hand_over_kernel, out_shape=shapes, in_specs=[HBM] * 9, ou...  3.4 us

profile of v4, /device:TPU:0, one launch (start us, length us, event | category | flops | bytes accessed | tf_op | source)
XLA Modules:
  0.0 122.3 jit_solution(3488041182348923725)
XLA Ops:
  0.6 118.1 %shard_map.196 = (bf16[256,1024]{1,0:T(8,128)(2,1)}, bf16[256,1024]{1,0:T(8,128)(2,1)}, bf16[128,1024]{1,0:T(8,128)(2,1)}, bf16[128,1024]{1,0:T(8,128)(2,1)}, f3...) custom-call(s32[16]{0:T(128)} %refs_0_.1, ...), custom_call_target="tpu_custom_call" | custom-call | tf_op jit(solution)/shard_map/pallas_call | solution.py:691
  118.8 3.4 %shard_map.197 = (bf16[256,1024]{1,0:T(8,128)(2,1)}, bf16[256,1024]{1,0:T(8,128)(2,1)}, bf16[128,1024]{1,0:T(8,128)(2,1)}, bf16[128,1024]{1,0:T(8,128)(2,1)}, f3...) custom-call(bf16[256,1024]{1,0:T(8,128)(2,1)} %get-tuple-element.27., ...), custom_call_target="tpu_custom_call" | custom-call | tf_op jit(solution)/shard_map/pallas_call | solution.py:704
